TPU v7x, 256 devices: a whole 4x4x8 slice. The times are simulated.
256 devices in a mesh: rep: 16 (over x, z_hi, core), tp: 16 (over z_lo, y).
Axes of the slice: x: 4, y: 4, z: 8 (z_hi: 2, z_lo: 4; z = z_hi * 4 + z_lo), core: 2. Of those that a mesh axis runs over, the one named last changes fastest.
Arguments:
- residual_in: bfloat16 [16384, 4608], P(('rep', 'tp'))
- attn_gain: float32 [4608], replicated, may hold values from 0.5 to 1.5
- branch_gain: float32 [4608], replicated, may hold values from 0.5 to 1.5
- w_query: bfloat16 [4608, 32, 128], P(None, 'tp'), may hold values from -0.09375 to 0.09375
- w_keyval: bfloat16 [4608, 16, 256], P(None, 'tp'), may hold values from -0.09375 to 0.09375
- w_out: bfloat16 [32, 128, 4608], P('tp'), may hold values from -0.09375 to 0.09375
- page_pool: bfloat16 [1536, 16, 16, 256], P('rep', None, 'tp'), may hold values from -320 to 320
- match_len: int32 [16, 4], P('rep'), may hold values from 1 to 512, as said below
- block_owner: int32 [16, 4, 32], P('rep'), may hold values from 0 to 15, as said below
- block_id: int32 [16, 4, 32], P('rep'), may hold values from 0 to 95
- suffix_len: int32 [16, 4], P('rep'), may hold values from 1 to 512, 1024 in all within a row
Outputs:
- layer_out: bfloat16 [16384, 4608], P(('rep', 'tp'))
Inputs may be any that keep to these rules, and one draw needn't show every extreme that they name: `match_len`: in every group some request has a cached prefix of exactly 512 tokens. `block_owner`: only entries with b * 16 < match_len of their request are read. Among the read blocks of one group at most 8 have the same owner, and in every group some owner holds exactly 8 of them.
All inputs are finite; a program needn't handle non-finite values.
Results may differ from a plain program's by a relative error of at most 0.012.
Values may be sent and summed in bfloat16 or wider, within the bound.
A program may use at most 128 MiB of HBM per device.

v0:
```python
import math

import jax
import jax.numpy as jnp
from jax import lax
from jax.sharding import PartitionSpec as P

score_scale = 1.0 / 12.0
soft_cap = 50.0


def rms_scale(values, gain):
    floats = values.astype(jnp.float32)
    mean_square = jnp.mean(floats * floats, axis=-1, keepdims=True)
    return floats * lax.rsqrt(mean_square + 1e-06) * gain


def rotate(values, position):
    half = values.shape[-1] // 2
    freq = jnp.exp(
        jnp.arange(half, dtype=jnp.float32) * (-2.0 * math.log(10000.0) / values.shape[-1])
    )
    angle = position.astype(jnp.float32)[:, None] * freq[None, :]
    cosine = jnp.cos(angle)[:, None, :]
    sine = jnp.sin(angle)[:, None, :]
    first = values[..., :half]
    second = values[..., half:]
    return jnp.concatenate(
        [first * cosine - second * sine, second * cosine + first * sine], axis=-1
    )


def score_part(query_rows, keys, values, visible):
    scores = (
        jnp.einsum("qksd,lkd->ksql", query_rows, keys, preferred_element_type=jnp.float32)
        * score_scale
    )
    capped = soft_cap * jnp.tanh(scores / soft_cap)
    weights = jnp.where(visible[None, None], jnp.exp(capped - soft_cap), 0.0)
    total = jnp.sum(weights, axis=-1)
    numer = jnp.einsum(
        "ksql,lkd->ksqd", weights.astype(jnp.bfloat16), values, preferred_element_type=jnp.float32
    )
    return (numer, total)


def per_device(
    residual_in,
    attn_gain,
    branch_gain,
    w_query,
    w_keyval,
    w_out,
    page_pool,
    match_len,
    block_owner,
    block_id,
    suffix_len,
):
    tok_dev, model_width = residual_in.shape
    groups = lax.axis_size("rep")
    tensor_ways = lax.axis_size("tp")
    suffix = tok_dev * tensor_ways
    heads_dev = w_query.shape[1]
    head_size = w_query.shape[2]
    kv_dev = w_keyval.shape[1]
    group_share = heads_dev // kv_dev
    requests = match_len.shape[1]
    blocks = block_owner.shape[2]
    block_len = page_pool.shape[1]
    pool_rows = page_pool.shape[0]
    entries = requests * blocks
    capacity = entries // groups
    normed = rms_scale(residual_in, attn_gain).astype(jnp.bfloat16)
    query_flat = w_query.reshape(model_width, heads_dev * head_size)
    keyval_flat = w_keyval.reshape(model_width, kv_dev * 2 * head_size)
    piece = lax.all_gather(normed, "tp", axis=0, tiled=True)
    projected = jnp.concatenate(
        [
            jnp.dot(piece, query_flat, preferred_element_type=jnp.float32),
            jnp.dot(piece, keyval_flat, preferred_element_type=jnp.float32),
        ],
        axis=1,
    )
    prefix_len = match_len[0]
    lengths = suffix_len[0]
    ends = jnp.cumsum(lengths)
    starts = ends - lengths
    token_index = jnp.arange(suffix, dtype=jnp.int32)
    request_of = jnp.sum((token_index[:, None] >= ends[None, :]).astype(jnp.int32), axis=1)
    request_hot = (request_of[:, None] == jnp.arange(requests, dtype=jnp.int32)[None, :]).astype(
        jnp.int32
    )
    position = jnp.sum(request_hot * (prefix_len - starts)[None, :], axis=1) + token_index
    query = rotate(
        projected[:, : heads_dev * head_size].reshape(suffix, heads_dev, head_size), position
    ).astype(jnp.bfloat16)
    keyval = projected[:, heads_dev * head_size :].reshape(suffix, kv_dev, 2 * head_size)
    key_suffix = rotate(keyval[..., :head_size], position).astype(jnp.bfloat16)
    val_suffix = keyval[..., head_size:].astype(jnp.bfloat16)
    entry_index = jnp.arange(entries, dtype=jnp.int32)
    entry_live = entry_index % blocks * block_len < jnp.repeat(prefix_len, blocks)
    owner_flat = block_owner[0].reshape(-1)
    ident_flat = block_id[0].reshape(-1)
    owner_hot = (
        (owner_flat[:, None] == jnp.arange(groups, dtype=jnp.int32)[None, :]) & entry_live[:, None]
    ).astype(jnp.int32)
    earlier = jnp.cumsum(owner_hot, axis=0) - owner_hot
    rank = jnp.sum(earlier * owner_hot, axis=1)
    slot_of = owner_flat * capacity + rank
    placed = ((slot_of[:, None] == entry_index[None, :]) & entry_live[:, None]).astype(jnp.int32)
    slot_request = jnp.sum(placed * (entry_index // blocks)[:, None], axis=0)
    slot_block = jnp.sum(placed * (entry_index % blocks)[:, None], axis=0)
    slot_live = jnp.sum(placed, axis=0) > 0
    slot_limit = jnp.sum(
        (slot_request[:, None] == jnp.arange(requests, dtype=jnp.int32)[None, :]).astype(jnp.int32)
        * prefix_len[None, :],
        axis=1,
    )
    everything = lax.all_gather(page_pool, "rep", axis=0, tiled=True)
    source_rows = jnp.sum(placed * (owner_flat * pool_rows + ident_flat)[:, None], axis=0)
    pages = jnp.take(everything, source_rows, axis=0)
    pages = pages.reshape(entries * block_len, kv_dev, 2 * head_size)
    key_prefix = pages[..., :head_size]
    val_prefix = pages[..., head_size:]
    key_request = jnp.repeat(slot_request, block_len)
    key_token = jnp.repeat(slot_block, block_len) * block_len + jnp.tile(
        jnp.arange(block_len, dtype=jnp.int32), entries
    )
    key_visible = jnp.repeat(slot_live, block_len) & (key_token < jnp.repeat(slot_limit, block_len))
    keys_joined = jnp.concatenate([key_prefix, key_suffix], axis=0)
    vals_joined = jnp.concatenate([val_prefix, val_suffix], axis=0)
    block_rows = min(512, suffix)
    block_count = suffix // block_rows

    def attend_block(index):
        first_row = index * block_rows
        rows_q = lax.dynamic_slice_in_dim(query, first_row, block_rows, 0).reshape(
            block_rows, kv_dev, group_share, head_size
        )
        request_q = lax.dynamic_slice_in_dim(request_of, first_row, block_rows, 0)
        token_q = lax.dynamic_slice_in_dim(token_index, first_row, block_rows, 0)
        prefix_mask = (request_q[:, None] == key_request[None, :]) & key_visible[None, :]
        suffix_mask = (request_q[:, None] == request_of[None, :]) & (
            token_index[None, :] <= token_q[:, None]
        )
        numer, total = score_part(
            rows_q, keys_joined, vals_joined, jnp.concatenate([prefix_mask, suffix_mask], axis=1)
        )
        result = (numer / total[..., None]).astype(jnp.bfloat16)
        return result.transpose(2, 0, 1, 3).reshape(block_rows, heads_dev * head_size)

    attended = lax.map(attend_block, jnp.arange(block_count, dtype=jnp.int32)).reshape(
        suffix, heads_dev * head_size
    )
    out_flat = w_out.reshape(heads_dev * head_size, model_width)
    branch = lax.psum_scatter(
        jnp.dot(attended, out_flat, preferred_element_type=jnp.float32).astype(jnp.bfloat16),
        "tp",
        scatter_dimension=0,
        tiled=True,
    ).astype(jnp.float32)
    return (residual_in.astype(jnp.float32) + rms_scale(branch, branch_gain)).astype(jnp.bfloat16)


def solution(mesh):
    placed = (
        P(("rep", "tp"), None),
        P(),
        P(),
        P(None, "tp", None),
        P(None, "tp", None),
        P("tp", None, None),
        P("rep", None, "tp", None),
        P("rep", None),
        P("rep", None, None),
        P("rep", None, None),
        P("rep", None),
    )
    return jax.shard_map(
        per_device, mesh=mesh, in_specs=placed, out_specs=P(("rep", "tp"), None), check_vma=False
    )
```

profile of v0, /device:TPU:40, one launch (start us, length us, event | category | flops | bytes accessed | tf_op | source)
XLA Modules:
  0.0 423.2 jit_solution(13284583521271281999)
XLA Ops:
  6.6 1.4 fusion.35
  8.0 2.1 fusion.37
  12.4 3.4 copy.39
  15.8 4.3 %copy.28 = bf16[256,4608]{1,0:T(8,128)(2,1)} copy(bf16[256,4608]{0,1:T(8,128)(2,1)} %bitcast.97) | data formatting | bytes 4718592 | tf_op jit(solution)/shard_map/dot_general | solution.py:80
  20.4 1.0 multiply_cosine_fusion.1
  21.4 100.2 %all-gather.3.cloned.1.call-done = bf16[1024,4608]{1,0:T(8,128)(2,1)} async-done(((bf16[64,4608]{1,0:T(8,128)(2,1)}), bf16[1024,4608]{1,0:T(8,128)(2,1)}) %all-gather.3.cloned.1.call-update) | async-done | bytes 9437200 | tf_op jit(solution)/shard_map/all_gather | solution.py:77
  121.7 6.0 %fusion.30 = f32[1024,1,256]{0,2,1:T(8,128)S(1)} fusion(bf16[1024,4608]{1,0:T(8,128)(2,1)} %all-gather.3.cloned.1.call-done, bf16[4608,1,256]{2,0,1:T(8,128)(2,1)} %param.17), kind=kOutput, calls=%fused_computation.37 | convolution fusion | flops 2415919104 | bytes 12845056 | tf_op jit(solution)/shard_map/dot_general | solution.py:81
  127.7 1.2 fusion.44
  129.7 0.8 copy.30
  130.5 5.9 %fusion.26 = f32[1024,2,128]{0,2,1:T(8,128)S(1)} fusion(bf16[2,128,4608]{2,1,0:T(8,128)(2,1)} %bitcast.100, bf16[1024,4608]{1,0:T(8,128)(2,1)} %all-gather.3.cloned.1.call-done), kind=kOutput, calls=%fused_computation.27 | convolution fusion | flops 2415919104 | bytes 12845056 | tf_op jit(solution)/shard_map/dot_general | solution.py:80
  137.5 127.5 %all-gather.5.cloned.1.call-done = bf16[1536,16,1,256]{3,1,2,0:T(8,128)(2,1)} async-done(((bf16[96,16,1,256]{3,1,2,0:T(8,128)(2,1)}), bf16[1536,16,1,256]{3,1,2,0:T(8,128)(2,1)}) %all-gather.5.cloned.1.call-update) | async-done | bytes 12582928 | tf_op jit(solution)/shard_map/all_gather | solution.py:120
  265.0 5.2 %gather_fusion = bf16[128,16,256]{2,1,0:T(8,128)(2,1)S(1)} fusion(bf16[1536,16,256]{2,1,0:T(8,128)(2,1)} %bitcast.102, s32[1024]{0:T(1024)S(1)} %pad_clamp_fusion), kind=kCustom, calls=%fused_computation | custom fusion | bytes 2097664 | tf_op jit(solution)/shard_map/jit(_take)/gather | solution.py:122
  270.8 0.9 fusion.53
  271.8 1.2 copy.32
  272.9 2.0 pad_maximum_fusion
  274.9 27.2 %while.14 = (s32[]{:T(128)}, bf16[2,512,256]{2,1,0:T(8,128)(2,1)}, s32[2]{0:T(128)S(1)}, s32[1024]{0:T(1024)S(1)}, s32[1024]{0:T(1024)S(1)}, /*index=5*/bf16[102...) while((s32[]{:T(128)}, bf16[2,512,256]{2,1,0:T(8,128)(2,1)}, ...), condition=%wide.region_13.14_spmd.clone.clone, body=%wide.region_11.13_spmd.clone.clone.sunk | while | flops 1647580160 | bytes 48832488 | solution.py:153
  278.4 5.4 %fusion.66 = (f32[2,512]{1,0:T(2,128)S(1)}, f32[512,2,3072]{2,0,1:T(8,128)S(1)}) fusion(pred[512,3072]{1,0:T(8,128)(4,1)S(1)} %pad_add_fusion.2, bf16[3072,1,128]{2,0,1:T(8,128)(2,1)S(1)} %copy-done.5, bf16[1024,2,128]{0,2,1:T(8,128)(2,1)S(1)} %copy-done.8, s32[]{:T(128)S(6)} %select_n.107), kind=kOutput, calls=%fused_computation.4.clone.1 | convolution fusion | flops 821033984 | bytes 15208452 | tf_op jit(solution)/shard_map/while/body/eval_jaxpr/qksd,lkd->ksql/dot_general | solution.py:35
  283.8 3.8 fusion.67
  292.0 5.4 %fusion.66 = (f32[2,512]{1,0:T(2,128)S(1)}, f32[512,2,3072]{2,0,1:T(8,128)S(1)}) fusion(pred[512,3072]{1,0:T(8,128)(4,1)S(1)} %pad_add_fusion.2, bf16[3072,1,128]{2,0,1:T(8,128)(2,1)S(1)} %copy-done.5, bf16[1024,2,128]{0,2,1:T(8,128)(2,1)S(1)} %copy-done.8, s32[]{:T(128)S(6)} %select_n.107), kind=kOutput, calls=%fused_computation.4.clone.1 | convolution fusion | flops 821033984 | bytes 15208452 | tf_op jit(solution)/shard_map/while/body/eval_jaxpr/qksd,lkd->ksql/dot_general | solution.py:35
  297.4 3.8 fusion.67
  302.2 6.0 %convolution_convert_fusion = bf16[1024,4608]{1,0:T(8,128)(2,1)} fusion(bf16[1024,256]{1,0:T(8,128)(2,1)} %bitcast.101, bf16[256,4608]{1,0:T(8,128)(2,1)S(1)} %bitcast.96), kind=kOutput, calls=%fused_computation.26 | convolution fusion | flops 2420637696 | bytes 12320768 | tf_op jit(solution)/shard_map/dot_general | solution.py:158
  308.2 105.0 %reduce-scatter.2.cloned.1.call-done = bf16[64,4608]{1,0:T(8,128)(2,1)} async-done(((bf16[1024,4608]{1,0:T(8,128)(2,1)}), bf16[64,4608]{1,0:T(8,128)(2,1)}) %reduce-scatter.2.cloned.1.call-update) | async-done | bytes 589840 | tf_op jit(solution)/shard_map/reduce_scatter | solution.py:157
  413.2 1.3 fusion.33
  414.6 2.2 fusion.38
  (105 shorter events, 12.4 us)
Async XLA Ops:
  6.5 295.6 %copy-start = (bf16[2,128,4608]{2,1,0:T(8,128)(2,1)S(1)}, bf16[2,128,4608]{2,1,0:T(8,128)(2,1)}, u32[]{:S(2)}) copy-start(bf16[2,128,4608]{2,1,0:T(8,128)(2,1)} %param.18) | copy-start | bytes 7077892
  6.5 4.4 %copy-start.12 = (s32[1,4]{1,0:T(1,128)S(1)}, s32[1,4]{1,0:T(1,128)}, u32[]{:S(2)}) copy-start(s32[1,4]{1,0:T(1,128)} %param.20) | copy-start | bytes 52
  6.5 4.6 %copy-start.10 = (s32[1,4,32]{2,1,0:T(4,128)S(1)}, s32[1,4,32]{2,1,0:T(4,128)}, u32[]{:S(2)}) copy-start(s32[1,4,32]{2,1,0:T(4,128)} %param.21) | copy-start | bytes 1540
  6.5 5.0 %copy-start.11 = (s32[1,4,32]{2,1,0:T(4,128)S(1)}, s32[1,4,32]{2,1,0:T(4,128)}, u32[]{:S(2)}) copy-start(s32[1,4,32]{2,1,0:T(4,128)} %param.22) | copy-start | bytes 1540
  6.5 5.6 %copy-start.13 = (s32[1,4]{1,0:T(1,128)S(1)}, s32[1,4]{1,0:T(1,128)}, u32[]{:S(2)}) copy-start(s32[1,4]{1,0:T(1,128)} %param.23) | copy-start | bytes 52
  6.5 115.1 %all-gather.3.cloned.1.call-start = ((), (), s32[]{:S(2)}) async-start(), calls=%async_computation.1 | async-start | bytes 10027008 | tf_op jit(solution)/shard_map/all_gather | solution.py:77
  10.2 254.9 %all-gather.5.cloned.1.call-start = ((), (), s32[]{:S(2)}) async-start(), calls=%async_computation.2 | async-start | bytes 13369344 | tf_op jit(solution)/shard_map/all_gather | solution.py:120
  10.9 402.3 %reduce-scatter.2.cloned.1.call-start = ((), (), s32[]{:S(2)}) async-start(), calls=%async_computation.3 | async-start | bytes 10027008 | tf_op jit(solution)/shard_map/reduce_scatter | solution.py:157
  270.3 1.4 copy-start.3
  270.8 2.1 copy-start.2
  276.3 1.8 copy-start.8
  277.2 1.2 copy-start.5
  278.4 5.4 %copy-start.4 = (bf16[3072,1,128]{0,2,1:T(8,128)(2,1)S(1)}, bf16[3072,1,128]{0,2,1:T(8,128)(2,1)}, u32[]{:S(2)}) copy-start(bf16[3072,1,128]{0,2,1:T(8,128)(2,1)} %get-tuple-element.396) | copy-start | bytes 2359300 | tf_op jit(solution)/shard_map/while
  283.8 3.9 copy-start.6
  287.8 0.8 copy-start.7
  289.9 1.8 copy-start.8
  290.8 1.2 copy-start.5
  292.0 5.4 %copy-start.4 = (bf16[3072,1,128]{0,2,1:T(8,128)(2,1)S(1)}, bf16[3072,1,128]{0,2,1:T(8,128)(2,1)}, u32[]{:S(2)}) copy-start(bf16[3072,1,128]{0,2,1:T(8,128)(2,1)} %get-tuple-element.396) | copy-start | bytes 2359300 | tf_op jit(solution)/shard_map/while
  297.4 3.9 copy-start.6
  301.4 0.8 copy-start.7
  308.2 106.3 %copy-start.1 = (bf16[64,4608]{1,0:T(8,128)(2,1)S(1)}, bf16[64,4608]{1,0:T(8,128)(2,1)}, u32[]{:S(2)}) copy-start(bf16[64,4608]{1,0:T(8,128)(2,1)} %param.13) | copy-start | bytes 1769476
  308.2 106.3 %copy-start.9 = (f32[4608]{0:T(1024)S(1)}, f32[4608]{0:T(1024)}, u32[]{:S(2)}) copy-start(f32[4608]{0:T(1024)} %param.15) | copy-start | bytes 55300
Sparse Core Ops, SparseCore 0:
  10.3 111.3 all-gather.2
  124.3 140.6 all-gather.4
  308.4 104.8 reduce-scatter.1
where the time goes:
time: 429 us; the launch traced here: 423 us
  waiting for transfers between devices  334 us (78%)
  matrix products  36.3 us (8%)
  local copies, waits for them, and re-layouts  21.8 us (5%)
  other arithmetic  16.7 us (4%)
  between operations  13.3 us (3%)
    all_gather x1, waiting for transfers between devices, per_device(): everything = lax.all_gather(page_pool, 'rep', axis=0, tiled=True)  128 us
    reduce_scatter x1, waiting for transfers between devices, per_device(): lax.psum_scatter(jnp.dot(attended, out_flat, preferred_element_type=jnp.f...  105 us
    all_gather x1, waiting for transfers between devices, per_device(): piece = lax.all_gather(normed, 'tp', axis=0, tiled=True)  100 us
    dot_general x2, matrix products, score_part(): jnp.einsum('qksd,lkd->ksql', query_rows, keys, preferred_element_type=jnp...  10.8 us
  transfers between devices with their start and end apart: 3, of which 3 were waited for; matrix products, arithmetic and copies ran while one was open for 6% of the time, Pallas kernels for 0%

commit v1 on v0

v1 whole, which is shorter than its diff:
```python
import functools
import math

import jax
import jax.numpy as jnp
from jax import lax
from jax.experimental import pallas as pl
from jax.experimental.pallas import tpu as pltpu
from jax.sharding import PartitionSpec as P

MESH = pl.DeviceIdType.MESH
F32 = jnp.float32
BF16 = jnp.bfloat16
I32 = jnp.int32

NZ = 4
NY = 4
NX = 4
NREP = 16
NTP = 16
D = 4608
TOK = 64
SUF = 1024
HD = 128
REQ = 4
NB = 32
BLK = 16
CAP = 8
POOL = 96
PIECE = 32
HALF = 32
NC = 3
CW = D // NC

NEAR = ((1, 2, 3), (0, 2, 3), (1, 3, 0), (2, 1, 0))


def pick(z, table):
    i0 = (1 - z) * (2 - z) * (3 - z) // 6
    i1 = z * (2 - z) * (3 - z) // 2
    i2 = z * (3 - z) * (z - 1) // 2
    i3 = z * (z - 1) * (z - 2) // 6
    return i0 * table[0] + i1 * table[1] + i2 * table[2] + i3 * table[3]


def remote(src, dst, send, recv, rep, tp):
    return pltpu.make_async_remote_copy(
        src_ref=src,
        dst_ref=dst,
        send_sem=send,
        recv_sem=recv,
        device_id=(rep, tp),
        device_id_type=MESH,
    )


def gather_kernel(
    res_ref,
    gain_ref,
    wq_hbm,
    wkv_hbm,
    wo_hbm,
    pool_ref,
    own_ref,
    id_ref,
    ml_ref,
    sl_ref,
    q_ref,
    k_ref,
    v_ref,
    pages_ref,
    wall_ref,
    g,
    wq_raw,
    w_all,
    tmp,
    ctab,
    stab,
    treq,
    rreq,
    sreq,
    sbuf,
    loc,
    zs,
    zr,
    zf,
    ys,
    yr,
    yhs,
    yhr,
    wzs,
    wzr,
    wzf,
    xs,
    xr,
    xhs,
    xhr,
    cs,
    cr,
    rqs,
    rqr,
    pgs,
    pgr,
):
    rep = lax.axis_index("rep")
    tp = lax.axis_index("tp")
    z = tp // NY
    y = tp % NY
    x = rep // 4
    zh = (rep // 2) % 2
    c = rep % 2

    def tp_of(zz, yy):
        return zz * NY + yy

    yn = (tp_of(z, (y + 1) % NY), tp_of(z, (y + 3) % NY))
    xn = (((x + 1) % NX * 2 + zh) * 2 + c, ((x + 3) % NX * 2 + zh) * 2 + c)
    other = (x * 2 + zh) * 2 + (1 - c)
    inner = (z * (3 - z)) > 0

    cp_wq = pltpu.make_async_copy(wq_hbm, wq_raw, loc.at[0])
    cp_wkv = pltpu.make_async_copy(wkv_hbm, w_all.at[:, pl.ds(256, 256)], loc.at[1])
    cp_wq.start()
    cp_wkv.start()

    barrier = pltpu.get_barrier_semaphore()

    @pl.when(z < 3)
    def _():
        pl.semaphore_signal(barrier, inc=1, device_id=(rep, tp + NY), device_id_type=MESH)

    @pl.when(z > 0)
    def _():
        pl.semaphore_signal(barrier, inc=1, device_id=(rep, tp - NY), device_id_type=MESH)

    for d in range(2):
        pl.semaphore_signal(barrier, inc=1, device_id=(rep, yn[d]), device_id_type=MESH)

    for d in range(1, NREP):
        pl.semaphore_signal(
            barrier, inc=1, device_id=((rep + d) % NREP, tp), device_id_type=MESH
        )

    xv = res_ref[...].astype(F32)
    ms = jnp.mean(xv * xv, axis=-1, keepdims=True)
    me = y * NZ + z
    g[me] = (xv * lax.rsqrt(ms + 1e-06) * gain_ref[...]).astype(BF16)

    pl.semaphore_wait(barrier, 2 + NREP - 1 + 1 + z * (3 - z) // 2)

    def zsend(d):
        to = tp + NY if d == 0 else tp - NY
        return (
            remote(g.at[me], g.at[me], zs.at[d], zr.at[z], rep, to),
            remote(
                wo_hbm.at[pl.ds((x * 2 + c) * PIECE, PIECE)],
                wall_ref.at[z, pl.ds((x * 2 + c) * PIECE, PIECE)],
                wzs.at[d],
                wzr.at[z],
                rep,
                to,
            ),
        )

    def ysend(d, zz):
        s = y * NZ + zz
        return remote(g.at[s], g.at[s], ys.at[d, zz], yr.at[d, zz], rep, yn[d])

    def yrecv(d, zz):
        s = (y + (3 if d == 0 else 1)) % NY * NZ + zz
        return remote(g.at[s], g.at[s], ys.at[d, zz], yr.at[d, zz], rep, yn[d])

    def yhalf(d, zz):
        s = (y + (3 if d == 0 else 1)) % NY * NZ + zz
        rows = pl.ds(d * HALF, HALF)
        return remote(g.at[s, rows], g.at[s, rows], yhs.at[d, zz], yhr.at[d, zz], rep, yn[d])

    def yhalf_recv(d, zz):
        s = (y + 2) % NY * NZ + zz
        rows = pl.ds(d * HALF, HALF)
        return remote(g.at[s, rows], g.at[s, rows], yhs.at[d, zz], yhr.at[d, zz], rep, yn[d])

    for d in range(2):
        ysend(d, z).start()

    @pl.when(z < 3)
    def _():
        a, b = zsend(0)
        a.start()
        b.start()

    @pl.when(z > 0)
    def _():
        a, b = zsend(1)
        a.start()
        b.start()

    o_iota = lax.broadcasted_iota(I32, (NREP, NB), 0)
    b_iota = lax.broadcasted_iota(I32, (1, NB), 1)
    b_up = lax.broadcasted_iota(I32, (NB, NB), 0)
    b_across = lax.broadcasted_iota(I32, (NB, NB), 1)
    owners = []
    columns = []
    for r in range(REQ):
        live = b_iota * BLK < ml_ref[0, r]
        owners.append(jnp.where(live, own_ref[r : r + 1, :], -1))
        columns.append(
            jnp.sum(jnp.where(b_up == b_across, owners[r], 0), axis=1, keepdims=True)
        )
    wanted = [jnp.zeros((NREP, NB), I32) for _ in range(CAP)]
    for r in range(REQ):
        same = (columns[r] == owners[r]) & (b_up < b_across)
        count = jnp.where(same, 1, 0)
        for e in range(r):
            count = count + jnp.where(columns[e] == owners[r], 1, 0)
        rank = jnp.sum(count, axis=0, keepdims=True)
        for s in range(CAP):
            hit = (owners[r] == o_iota) & (rank == s)
            wanted[s] = wanted[s] + jnp.where(hit, id_ref[r : r + 1, :], 0)
    slot_iota = lax.broadcasted_iota(I32, (NREP, 128), 1)
    table = jnp.zeros((NREP, 128), I32)
    for s in range(CAP):
        table = table + jnp.where(
            slot_iota == s, jnp.sum(wanted[s], axis=1, keepdims=True), 0
        )
    treq[...] = jnp.broadcast_to(table[:, None, :], (NREP, 8, 128))
    rreq[rep] = treq[rep]

    def rq_send(d):
        to = (rep + d) % NREP
        return remote(treq.at[to], rreq.at[rep], rqs.at[d], rqr.at[d], to, tp)

    def rq_recv(d):
        frm = (rep + NREP - d) % NREP
        return remote(treq.at[frm], rreq.at[frm], rqs.at[d], rqr.at[d], frm, tp)

    def pg_send(d):
        to = (rep + d) % NREP
        return remote(sbuf.at[to], pages_ref.at[rep], pgs.at[d], pgr.at[d], to, tp)

    def pg_recv(d):
        frm = (rep + NREP - d) % NREP
        return remote(sbuf.at[frm], pages_ref.at[frm], pgs.at[d], pgr.at[d], frm, tp)

    def each(n0, n1, f):
        def body(i, carry):
            f(i)
            return carry

        lax.fori_loop(n0, n1, body, 0)

    each(1, NREP, lambda d: rq_send(d).start())
    each(1, NREP, lambda d: rq_recv(d).wait_recv())
    cp_req = pltpu.make_async_copy(rreq, sreq, loc.at[2])
    cp_req.start()
    cp_req.wait()

    def fill(d):
        to = (rep + d) % NREP
        for s in range(CAP):
            sbuf[to, pl.ds(s * BLK, BLK), :] = pool_ref[jnp.clip(sreq[to, 0, s], 0, POOL - 1)]

        @pl.when(d > 0)
        def _():
            pg_send(d).start()

    each(0, NREP, fill)
    cp_page = pltpu.make_async_copy(sbuf.at[rep], pages_ref.at[rep], loc.at[3])
    cp_page.start()

    e0 = sl_ref[0, 0]
    e1 = e0 + sl_ref[0, 1]
    e2 = e1 + sl_ref[0, 2]

    def tables(i):
        tok = i * 128 + lax.broadcasted_iota(I32, (128, HD), 0)
        off = jnp.where(tok >= e0, ml_ref[0, 1] - e0, ml_ref[0, 0])
        off = jnp.where(tok >= e1, ml_ref[0, 2] - e1, off)
        off = jnp.where(tok >= e2, ml_ref[0, 3] - e2, off)
        lane = lax.broadcasted_iota(I32, (128, HD), 1)
        low = lane < HD // 2
        freq = jnp.exp(
            jnp.where(low, lane, lane - HD // 2).astype(F32) * (-2.0 * math.log(10000.0) / HD)
        )
        angle = (tok + off).astype(F32) * freq
        rows = pl.ds(pl.multiple_of(i * 128, 128), 128)
        ctab[rows, :] = jnp.cos(angle)
        sine = jnp.sin(angle)
        stab[rows, :] = jnp.where(low, -sine, sine)

    each(0, SUF // 128, tables)

    cp_wq.wait()

    def split(i):
        rows = pl.ds(pl.multiple_of(i * 1024, 1024), 1024)
        tmp[0:1024, :] = wq_raw[rows, :].astype(F32)
        dst = pl.ds(pl.multiple_of(i * 512, 512), 512)
        w_all[dst, 0:128] = tmp[pl.ds(0, 512, stride=2), :].astype(BF16)
        w_all[dst, 128:256] = tmp[pl.ds(1, 512, stride=2), :].astype(BF16)

    each(0, 9, split)
    cp_wkv.wait()

    def project(col):
        rows = g[pl.ds(col * NZ, NZ)].reshape(NZ * TOK, D)
        out = jnp.dot(rows, w_all[...], preferred_element_type=F32)
        for zz in range(NZ):
            at = pl.ds(pl.multiple_of((zz * NY + col) * TOK, TOK), TOK)
            cosine = ctab[at, :]
            sine = stab[at, :]
            part = out[zz * TOK : (zz + 1) * TOK]
            for h in range(3):
                vals = part[:, h * HD : (h + 1) * HD]
                turned = (vals * cosine + pltpu.roll(vals, HD // 2, 1) * sine).astype(BF16)
                if h < 2:
                    q_ref[at, h * HD : (h + 1) * HD] = turned
                else:
                    k_ref[at, :] = turned
            v_ref[at, :] = part[:, 3 * HD :].astype(BF16)

    def rows_of(xx, cc):
        return (xx * 2 + cc) * PIECE

    def wx(d, zz, frm):
        at = wall_ref.at[zz, pl.ds(rows_of(frm, c), PIECE)]
        return remote(at, at, xs.at[d, zz], xr.at[d, zz], xn[d], tp)

    def wxh(d, zz, frm):
        at = wall_ref.at[zz, pl.ds(rows_of(frm, c) + d * (PIECE // 2), PIECE // 2)]
        return remote(at, at, xhs.at[d, zz], xhr.at[d, zz], xn[d], tp)

    def wc(n, zz, frm, cc, first, count):
        at = wall_ref.at[zz, pl.ds(rows_of(frm, cc) + first, count)]
        return remote(at, at, cs.at[n, zz], cr.at[n, zz], other, tp)

    def core_parts(cc):
        h = PIECE // 2
        return (
            (x, cc, 0, PIECE),
            ((x + 3) % NX, cc, 0, PIECE),
            ((x + 1) % NX, cc, 0, PIECE),
            ((x + 2) % NX, cc, 0, h),
            ((x + 2) % NX, cc, h, h),
        )

    def core_send(n, zz):
        return wc(n, zz, *core_parts(c)[n])

    def core_recv(n, zz):
        return wc(n, zz, *core_parts(1 - c)[n])

    near = [pick(z, [NEAR[k][j] for k in range(4)]) for j in range(3)]
    way = [pick(z, [0, (1, -1, -1)[j], (1, -1, 1)[j], 0]) for j in range(3)]

    def zfwd(j):
        s = y * NZ + near[j]
        return remote(g.at[s], g.at[s], zf.at[j], zr.at[near[j]], rep, tp + NY * way[j])

    def wzfwd(j):
        at = wall_ref.at[near[j], pl.ds(rows_of(x, c), PIECE)]
        return remote(at, at, wzf.at[j], wzr.at[near[j]], rep, tp + NY * way[j])

    def zstep(j):
        s = y * NZ + near[j]
        remote(g.at[s], g.at[s], zf.at[j], zr.at[near[j]], rep, yn[0]).wait_recv()

        @pl.when(inner)
        def _():
            zfwd(j).start()

        for d in range(2):
            ysend(d, near[j]).start()

    def wzstep(j):
        at = wall_ref.at[near[j], pl.ds(rows_of(x, c), PIECE)]
        remote(at, at, wzf.at[j], wzr.at[near[j]], rep, yn[0]).wait_recv()

        @pl.when(inner)
        def _():
            wzfwd(j).start()

        for d in range(2):
            wx(d, near[j], x).start()
        core_send(0, near[j]).start()

    def ystep(zz):
        for d in range(2):
            yrecv(d, zz).wait_recv()
            yhalf(d, zz).start()

    def xstep(j):
        zz = near[j]
        for d in range(2):
            frm = (x + (3 if d == 0 else 1)) % NX
            wx(d, zz, frm).wait_recv()
            wxh(d, zz, frm).start()
            core_send(1 + d, zz).start()

    def xhstep(j):
        zz = near[j]
        for d in range(2):
            wxh(d, zz, (x + 2) % NX).wait_recv()
            core_send(3 + d, zz).start()

    zstep(0)
    wzstep(0)
    ystep(z)
    zstep(1)
    wzstep(1)
    xstep(0)
    ystep(near[0])
    zstep(2)
    wzstep(2)
    xhstep(0)
    xstep(1)
    project(y)
    ystep(near[1])
    xhstep(1)
    xstep(2)
    ystep(near[2])
    project((y + 1) % NY)
    project((y + 3) % NY)
    xhstep(2)
    for zz in [z] + near:
        for d in range(2):
            yhalf_recv(d, zz).wait_recv()
    project((y + 2) % NY)

    cp_page.wait()
    each(1, NREP, lambda d: pg_recv(d).wait_recv())
    for j in range(3):
        for n in range(5):
            core_recv(n, near[j]).wait_recv()
    each(1, NREP, lambda d: rq_send(d).wait_send())
    each(1, NREP, lambda d: pg_send(d).wait_send())

    @pl.when(z < 3)
    def _():
        a, b = zsend(0)
        a.wait_send()
        b.wait_send()

    @pl.when(z > 0)
    def _():
        a, b = zsend(1)
        a.wait_send()
        b.wait_send()

    for zz in [z] + near:
        for d in range(2):
            ysend(d, zz).wait_send()
            yhalf(d, zz).wait_send()
    for j in range(3):

        @pl.when(inner)
        def _():
            zfwd(j).wait_send()
            wzfwd(j).wait_send()

        zz = near[j]
        for d in range(2):
            wx(d, zz, x).wait_send()
            wxh(d, zz, (x + (3 if d == 0 else 1)) % NX).wait_send()
        for n in range(5):
            core_send(n, zz).wait_send()


def attend_kernel(
    q_ref, k_ref, v_ref, pages_ref, own_ref, ml_ref, sl_ref, o_ref, kpre, vpre, vsuf, acc, cnt
):
    rows_blk = 128
    keys_blk = 256
    scale = 1.0 / 600.0
    power = 50.0 / math.log(2.0)
    vsuf[:, :HD] = v_ref[...]
    vsuf[:, HD:] = jnp.ones((SUF, HD), BF16)
    vpre[:, HD:] = jnp.ones((REQ * NB * BLK, HD), BF16)
    for o in range(NREP):
        cnt[o] = 0
    for r in range(REQ):
        blocks = (ml_ref[0, r] + BLK - 1) // BLK
        padded = (ml_ref[0, r] + keys_blk - 1) // keys_blk * (keys_blk // BLK)

        def place(b, carry):
            o = own_ref[r, b]
            s = cnt[o]
            cnt[o] = s + 1
            page = pages_ref[o, pl.ds(pl.multiple_of(s * BLK, BLK), BLK), :]
            at = pl.ds(pl.multiple_of(r * NB * BLK + b * BLK, BLK), BLK)
            kpre[at, :] = page[:, :HD]
            vpre[at, :HD] = page[:, HD:]
            return carry

        def clear(b, carry):
            at = pl.ds(pl.multiple_of(r * NB * BLK + b * BLK, BLK), BLK)
            kpre[at, :] = jnp.zeros((BLK, HD), BF16)
            vpre[at, :HD] = jnp.zeros((BLK, HD), BF16)
            return carry

        lax.fori_loop(0, blocks, place, 0)
        lax.fori_loop(blocks, padded, clear, 0)

    starts = [0]
    for r in range(REQ):
        starts.append(starts[-1] + sl_ref[0, r])

    def weigh(q2, keys):
        scores = lax.dot_general(q2, keys, (((1,), (1,)), ((), ())), preferred_element_type=F32)
        return jnp.exp2(jnp.tanh(scores * scale) * power)

    def block(i, carry):
        t0 = i * rows_blk
        at = pl.ds(pl.multiple_of(t0, rows_blk), rows_blk)
        q2 = jnp.concatenate([q_ref[at, :HD], q_ref[at, HD:]], axis=0)
        row = lax.broadcasted_iota(I32, (2 * rows_blk, 1), 0)
        tok = t0 + jnp.where(row >= rows_blk, row - rows_blk, row)
        lane = lax.broadcasted_iota(I32, (2 * rows_blk, keys_blk), 1)
        acc[...] = jnp.zeros_like(acc)
        first = 0
        row_start = jnp.zeros_like(tok)
        for r in range(1, REQ):
            first = jnp.where(t0 >= starts[r], starts[r], first)
            row_start = jnp.where(tok >= starts[r], starts[r], row_start)
        for r in range(REQ):

            @pl.when((starts[r] < t0 + rows_blk) & (starts[r + 1] > t0))
            def _():
                limit = jnp.where((tok >= starts[r]) & (tok < starts[r + 1]), ml_ref[0, r], 0)

                def chunk(ch, inner_carry):
                    keys = pl.ds(
                        pl.multiple_of(r * NB * BLK + ch * keys_blk, keys_blk), keys_blk
                    )
                    w = weigh(q2, kpre[keys, :])
                    w = jnp.where(lane < limit - ch * keys_blk, w, 0.0).astype(BF16)
                    acc[...] += jnp.dot(w, vpre[keys, :], preferred_element_type=F32)
                    return inner_carry

                lax.fori_loop(0, (ml_ref[0, r] + keys_blk - 1) // keys_blk, chunk, 0)

        def own_chunk(ch, inner_carry):
            keys = pl.ds(pl.multiple_of(ch * keys_blk, keys_blk), keys_blk)
            w = weigh(q2, k_ref[keys, :])
            key = lane + ch * keys_blk
            w = jnp.where((key >= row_start) & (key <= tok), w, 0.0).astype(BF16)
            acc[...] += jnp.dot(w, vsuf[keys, :], preferred_element_type=F32)
            return inner_carry

        lax.fori_loop(first // keys_blk, (t0 + rows_blk - 1) // keys_blk + 1, own_chunk, 0)
        done = (acc[:, :HD] / acc[:, HD:]).astype(BF16)
        o_ref[at, :HD] = done[:rows_blk]
        o_ref[at, HD:] = done[rows_blk:]
        return carry

    lax.fori_loop(0, SUF // rows_blk, block, 0)


def output_kernel(
    att_ref,
    wo_hbm,
    wall_hbm,
    res_ref,
    gain_ref,
    out_ref,
    a,
    w,
    p,
    rel,
    sb,
    rx,
    br,
    loc,
    asm,
    arm,
    hs,
    hr,
    os,
    orr,
    ss,
    sr,
):
    rep = lax.axis_index("rep")
    tp = lax.axis_index("tp")
    z = tp // NY
    y = tp % NY
    rows = NY * TOK
    yn = (z * NY + (y + 1) % NY, z * NY + (y + 3) % NY)

    def wload(d):
        zz = (z + d) % NZ
        src = wo_hbm if d == 0 else wall_hbm.at[zz]
        return pltpu.make_async_copy(src, w.at[d], loc.at[d])

    for d in range(NZ):
        wload(d).start()

    barrier = pltpu.get_barrier_semaphore()
    for d in range(1, NZ):
        pl.semaphore_signal(
            barrier, inc=1, device_id=(rep, (z + d) % NZ * NY + y), device_id_type=MESH
        )
    for d in range(2):
        pl.semaphore_signal(barrier, inc=1, device_id=(rep, yn[d]), device_id_type=MESH)
    pl.semaphore_wait(barrier, NZ - 1 + 2)

    def asend(d):
        to = (z + d) % NZ
        return remote(
            att_ref.at[pl.ds(to * rows, rows)], a.at[NZ - d], asm.at[d], arm.at[NZ - d], rep,
            to * NY + y,
        )

    def arecv(d):
        return remote(a.at[d], a.at[d], asm.at[d], arm.at[d], rep, yn[0])

    for d in range(1, NZ):
        asend(d).start()
    a[0] = att_ref[pl.ds(pl.multiple_of(z * rows, rows), rows), :]
    for d in range(NZ):
        wload(d).wait()
    for d in range(1, NZ):
        arecv(d).wait_recv()

    up = ((y + 1) % NY, (y + 3) % NY)
    far = (y + 2) % NY

    def via(d, n):
        at = pl.ds(d * HALF, HALF)
        return remote(p.at[n, far, at], rel.at[d, n], hs.at[d, n], hr.at[d, n], rep, yn[d])

    def straight(d, n):
        at = pl.ds((1 - d) * HALF, HALF)
        return remote(p.at[n, up[d], at], rx.at[d, n, at], os.at[d, n], orr.at[d, n], rep, yn[d])

    def summed(d, n):
        at = pl.ds(d * HALF, HALF)
        return remote(sb.at[d, n], rx.at[d, n, at], ss.at[d, n], sr.at[d, n], rep, yn[d])

    for n in range(NC):
        total = jnp.dot(a[0], w[0, :, n * CW : (n + 1) * CW], preferred_element_type=F32)
        for d in range(1, NZ):
            total += jnp.dot(a[d], w[d, :, n * CW : (n + 1) * CW], preferred_element_type=F32)
        p[n] = total.astype(BF16).reshape(NY, TOK, CW)
        for d in range(2):
            via(d, n).start()
        for d in range(2):
            straight(d, n).start()
    for n in range(NC):
        for d in range(2):
            via(d, n).wait_recv()
            at = pl.ds(d * HALF, HALF)
            sb[d, n] = (p[n, up[d], at].astype(F32) + rel[d, n].astype(F32)).astype(BF16)
            summed(d, n).start()
    square = jnp.zeros((TOK, 1), F32)
    for n in range(NC):
        for d in range(2):
            straight(d, n).wait_recv()
            summed(d, n).wait_recv()
        total = p[n, y].astype(F32) + rx[0, n].astype(F32) + rx[1, n].astype(F32)
        br[n] = total
        square += jnp.sum(total * total, axis=-1, keepdims=True)
    inv = lax.rsqrt(square * (1.0 / D) + 1e-06)
    for n in range(NC):
        at = slice(n * CW, (n + 1) * CW)
        out_ref[:, at] = (
            res_ref[:, at].astype(F32) + br[n] * inv * gain_ref[:, at]
        ).astype(BF16)
    for d in range(1, NZ):
        asend(d).wait_send()
    for n in range(NC):
        for d in range(2):
            via(d, n).wait_send()
            straight(d, n).wait_send()
            summed(d, n).wait_send()


VM = pl.BlockSpec(memory_space=pltpu.VMEM)
SM = pl.BlockSpec(memory_space=pltpu.SMEM)
ANY = pl.BlockSpec(memory_space=pl.ANY)


def dma(*shape):
    return pltpu.SemaphoreType.DMA(shape)


def per_device(
    residual_in,
    attn_gain,
    branch_gain,
    w_query,
    w_keyval,
    w_out,
    page_pool,
    match_len,
    block_owner,
    block_id,
    suffix_len,
):
    wq = w_query.reshape(2 * D, HD)
    wkv = w_keyval.reshape(D, 2 * HD)
    wo = w_out.reshape(2 * HD, D)
    pool = page_pool.reshape(POOL, BLK, 2 * HD)
    owner = block_owner.reshape(REQ, NB)
    ident = block_id.reshape(REQ, NB)
    query, key, value, pages, wall = pl.pallas_call(
        gather_kernel,
        out_shape=(
            jax.ShapeDtypeStruct((SUF, 2 * HD), BF16),
            jax.ShapeDtypeStruct((SUF, HD), BF16),
            jax.ShapeDtypeStruct((SUF, HD), BF16),
            jax.ShapeDtypeStruct((NREP, CAP * BLK, 2 * HD), BF16),
            jax.ShapeDtypeStruct((NZ, 2 * HD, D), BF16),
        ),
        in_specs=[VM, VM, ANY, ANY, ANY, VM, VM, VM, SM, SM],
        out_specs=(VM, VM, VM, ANY, ANY),
        scratch_shapes=[
            pltpu.VMEM((NTP, TOK, D), BF16),
            pltpu.VMEM((2 * D, HD), BF16),
            pltpu.VMEM((D, 4 * HD), BF16),
            pltpu.VMEM((1032, HD), F32),
            pltpu.VMEM((SUF, HD), F32),
            pltpu.VMEM((SUF, HD), F32),
            pltpu.VMEM((NREP, 8, 128), I32),
            pltpu.VMEM((NREP, 8, 128), I32),
            pltpu.SMEM((NREP, 8, 128), I32),
            pltpu.VMEM((NREP, CAP * BLK, 2 * HD), BF16),
            dma(4),
            dma(2),
            dma(NZ),
            dma(3),
            dma(2, NZ),
            dma(2, NZ),
            dma(2, NZ),
            dma(2, NZ),
            dma(2),
            dma(NZ),
            dma(3),
            dma(2, NZ),
            dma(2, NZ),
            dma(2, NZ),
            dma(2, NZ),
            dma(5, NZ),
            dma(5, NZ),
            dma(NREP),
            dma(NREP),
            dma(NREP),
            dma(NREP),
        ],
        compiler_params=pltpu.CompilerParams(
            collective_id=0, has_side_effects=True, vmem_limit_bytes=44 << 20
        ),
        name="gather_project",
    )(
        residual_in,
        attn_gain.reshape(1, D),
        wq,
        wkv,
        wo,
        pool,
        owner,
        ident,
        match_len,
        suffix_len,
    )
    attended = pl.pallas_call(
        attend_kernel,
        out_shape=jax.ShapeDtypeStruct((SUF, 2 * HD), BF16),
        in_specs=[VM, VM, VM, VM, SM, SM, SM],
        out_specs=VM,
        scratch_shapes=[
            pltpu.VMEM((REQ * NB * BLK, HD), BF16),
            pltpu.VMEM((REQ * NB * BLK, 2 * HD), BF16),
            pltpu.VMEM((SUF, 2 * HD), BF16),
            pltpu.VMEM((256, 256), F32),
            pltpu.SMEM((NREP,), I32),
        ],
        compiler_params=pltpu.CompilerParams(vmem_limit_bytes=32 << 20),
        name="attend",
    )(query, key, value, pages, owner, match_len, suffix_len)
    return pl.pallas_call(
        output_kernel,
        out_shape=jax.ShapeDtypeStruct((TOK, D), BF16),
        in_specs=[VM, ANY, ANY, VM, VM],
        out_specs=VM,
        scratch_shapes=[
            pltpu.VMEM((NZ, NY * TOK, 2 * HD), BF16),
            pltpu.VMEM((NZ, 2 * HD, D), BF16),
            pltpu.VMEM((NC, NY, TOK, CW), BF16),
            pltpu.VMEM((2, NC, HALF, CW), BF16),
            pltpu.VMEM((2, NC, HALF, CW), BF16),
            pltpu.VMEM((2, NC, TOK, CW), BF16),
            pltpu.VMEM((NC, TOK, CW), F32),
            dma(NZ),
            dma(NZ),
            dma(NZ),
            dma(2, NC),
            dma(2, NC),
            dma(2, NC),
            dma(2, NC),
            dma(2, NC),
            dma(2, NC),
        ],
        compiler_params=pltpu.CompilerParams(
            collective_id=1, has_side_effects=True, vmem_limit_bytes=44 << 20
        ),
        name="project_out",
    )(attended, wo, wall, residual_in, branch_gain.reshape(1, D))


def solution(mesh):
    placed = (
        P(("rep", "tp"), None),
        P(),
        P(),
        P(None, "tp", None),
        P(None, "tp", None),
        P("tp", None, None),
        P("rep", None, "tp", None),
        P("rep", None),
        P("rep", None, None),
        P("rep", None, None),
        P("rep", None),
    )
    return jax.shard_map(
        per_device, mesh=mesh, in_specs=placed, out_specs=P(("rep", "tp"), None), check_vma=False
    )
```

time: 429 us -> 183 us (0.43); the launches traced: 423 us -> 183 us
  waiting for transfers between devices: 334 us -> 0 us
  Pallas kernels: 0 us -> 173 us
  matrix products: 36.3 us -> 0 us
  other arithmetic: 16.7 us -> 0 us
  between operations: 13.3 us -> 0.08 us
  local copies, waits for them, and re-layouts: 21.8 us -> 9.78 us
    all_gather x2 -> x0, waiting for transfers between devices: 228 us -> none  [the longest x1 128 us: per_device(): everything = lax.all_gather(page_pool, 'rep', axis=0, tiled=True)]
    pallas_call x0 -> x3, Pallas kernels: none -> 173 us  [the longest x1 106 us: per_device(): pl.pallas_call(gather_kernel, out_shape=(jax.ShapeDtypeStruct((SUF, 2 * H...]
    reduce_scatter x1 -> x0, waiting for transfers between devices: 105 us -> none  [per_device(): lax.psum_scatter(jnp.dot(attended, out_flat, preferred_element_type=jnp.f...]
    dot_general x7 -> x0, matrix products: 36.3 us -> none  [the longest x2 10.8 us: score_part(): jnp.einsum('qksd,lkd->ksql', query_rows, keys, preferred_element_type=jnp...]
    gather x1 -> x0, local copies, waits for them, and re-layouts: 5.22 us -> none  [per_device(): pages = jnp.take(everything, source_rows, axis=0)]
    unnamed x20 -> x21, local copies, waits for them, and re-layouts: 4.64 us -> 9.02 us
    convert_element_type x4 -> x0, other arithmetic: 4.36 us -> none  [the longest x1 2.16 us: per_device(): (residual_in.astype(jnp.float32) + rms_scale(branch, branch_gain)).astype...]
    dot_general x1 -> x0, local copies, waits for them, and re-layouts: 4.32 us -> none  [per_device(): jnp.dot(piece, query_flat, preferred_element_type=jnp.float32)]
  transfers between devices with their start and end apart: 3 -> 0, of which waited for: 3 -> 0; matrix products, arithmetic and copies ran while one was open for 6% -> 0% of each run, Pallas kernels for 0% -> 0%
where the time goes in v1:
time: 183 us
  Pallas kernels  173 us (95%)
  local copies, waits for them, and re-layouts  9.78 us (5%)
    pallas_call x1, Pallas kernels, per_device(): pl.pallas_call(gather_kernel, out_shape=(jax.ShapeDtypeStruct((SUF, 2 * H...  106 us
    pallas_call x1, Pallas kernels, per_device(): pl.pallas_call(output_kernel, out_shape=jax.ShapeDtypeStruct((TOK, D), BF...  52.3 us
    pallas_call x1, Pallas kernels, per_device(): pl.pallas_call(attend_kernel, out_shape=jax.ShapeDtypeStruct((SUF, 2 * HD...  14.4 us
    unnamed x21, local copies, waits for them, and re-layouts  9.02 us

profile of v1, /device:TPU:40, one launch (start us, length us, event | category | flops | bytes accessed | tf_op | source)
XLA Modules:
  0.0 182.9 jit_solution(904743561756248040)
XLA Ops:
  0.0 0.7 reshape.24.gain_ref
  0.7 0.0 copy-start.1
  0.8 1.1 copy-done.1
  1.8 0.0 copy-start.2
  1.8 1.7 copy-done.2
  3.5 0.0 copy-start.3
  3.5 1.7 copy-done.3
  5.1 0.0 copy-start.4
  5.1 1.1 copy-done.4
  6.3 0.0 copy-start.5
  6.3 0.7 copy-done.5
  7.0 0.0 copy-start.6
  7.0 0.7 copy-done.6
  7.6 0.0 copy-start.7
  7.6 0.7 copy-done.7
  8.3 0.7 copy-done.8
  9.0 106.3 %gather_project.1 = (bf16[1024,256]{1,0:T(8,128)(2,1)S(1)}, bf16[1024,128]{1,0:T(8,128)(2,1)S(1)}, bf16[1024,128]{1,0:T(8,128)(2,1)S(1)}, bf16[16,128,256]{2,1,0:T(8,128)(2,1)S(1)}, bf16[4,256,4608]{2,1,0:T(8,128)(2,1)}) custom-call(bf16[64,4608]{1,0:T(8,128)(2,1)S(1)} %copy-done.1, f32[1,4608]{1,0:T(1,128)S(1)} %reshape.24.gain_ref, ...), custom_call_target="tpu_custom_call" | custom-call | tf_op jit(solution)/shard_map/gather_project/pallas_call | solution.py:706
  115.3 0.0 copy-start.9
  115.3 0.0 copy-start
  115.3 14.4 %attend.1.att_ref = bf16[1024,256]{1,0:T(8,128)(2,1)S(1)} custom-call(bf16[1024,256]{1,0:T(8,128)(2,1)S(1)} %get-tuple-element.10.q_ref, bf16[1024,128]{1,0:T(8,128)(2,1)S(1)} %get-tuple-element.11.k_ref, bf16[1024,128]{1,0:T(8,128)(2,1)S(1)} %get-tuple-element.12.v_ref, bf16[16,128,256]{2,1,0:T(8,128)(2,1)S(1)} %get-tuple-element.13.pages_ref, ...), custom_call_target="tpu_custom_call" | custom-call | tf_op jit(solution)/shard_map/attend/pallas_call | solution.py:766
  129.7 0.0 copy-done.9
  129.7 0.0 copy-done
  129.7 52.3 %project_out.1 = bf16[64,4608]{1,0:T(8,128)(2,1)S(1)} custom-call(bf16[1024,256]{1,0:T(8,128)(2,1)S(1)} %attend.1.att_ref, bf16[256,4608]{1,0:T(8,128)(2,1)S(1)} %bitcast.7, bf16[4,256,4608]{2,1,0:T(8,128)(2,1)} %get-tuple-element.14.wall_hbm, bf16[64,4608]{1,0:T(8,128)(2,1)S(1)} %copy-done.1, f32[1,4608]{1,0:T(1,128)S(1)} %reshape.31.gain_ref), custom_call_target="tpu_custom_call" | custom-call | tf_op jit(solution)/shard_map/project_out/pallas_call | solution.py:781
  182.1 0.8 copy.13
  (2 shorter events, 0.0 us)
Async XLA Ops:
  0.7 1.1 copy-start.1
  1.8 1.7 copy-start.2
  3.5 1.7 copy-start.3
  5.1 1.1 copy-start.4
  6.3 0.7 copy-start.5
  7.0 0.7 copy-start.6
  7.6 0.7 copy-start.7
  8.3 0.7 copy-start.8
  115.3 14.4 %copy-start.9 = (f32[4608]{0:T(1024)S(1)}, f32[4608]{0:T(1024)}, u32[]{:S(2)}) copy-start(f32[4608]{0:T(1024)} %param.13) | copy-start | bytes 55300
  115.3 14.4 %copy-start = (bf16[2,128,4608]{2,1,0:T(8,128)(2,1)S(1)}, bf16[2,128,4608]{2,1,0:T(8,128)(2,1)}, u32[]{:S(2)}) copy-start(bf16[2,128,4608]{2,1,0:T(8,128)(2,1)} %param.16) | copy-start | bytes 7077892

commit v2 on v1

v2 whole, which is shorter than its diff:
```python
import functools
import math

import jax
import jax.numpy as jnp
from jax import lax
from jax.experimental import pallas as pl
from jax.experimental.pallas import tpu as pltpu
from jax.sharding import PartitionSpec as P

MESH = pl.DeviceIdType.MESH
F32 = jnp.float32
BF16 = jnp.bfloat16
I32 = jnp.int32

NZ = 4
NY = 4
NX = 4
NREP = 16
NTP = 16
D = 4608
TOK = 64
SUF = 1024
HD = 128
REQ = 4
NB = 32
BLK = 16
CAP = 8
POOL = 96
WROWS = (576, 1152, 32, 32, 32)
HALF = 32
NC = 3
CW = D // NC

def remote(src, dst, send, recv, rep, tp):
    return pltpu.make_async_remote_copy(
        src_ref=src,
        dst_ref=dst,
        send_sem=send,
        recv_sem=recv,
        device_id=(rep, tp),
        device_id_type=MESH,
    )


def gather_kernel(
    res_hbm,
    gain_ref,
    wq_hbm,
    wkv_hbm,
    wo_hbm,
    pool_hbm,
    own_hbm,
    id_hbm,
    ml_hbm,
    sl_hbm,
    qkv_ref,
    pages_ref,
    wall_ref,
    res,
    pool,
    own_ref,
    id_ref,
    ml_ref,
    sl_ref,
    g,
    raw1,
    raw2,
    w1,
    w2,
    tmp,
    ctab,
    stab,
    ex,
    exr,
    treq,
    rreq,
    sreq,
    sbuf,
    loc,
    ts,
    tr,
    ys,
    yr,
    yhs,
    yhr,
    wis,
    wir,
    zs,
    zr,
    zhs,
    zhr,
    xs,
    xr,
    xhs,
    xhr,
    cs,
    cr,
    es,
    er,
    rqs,
    rqr,
    pgs,
    pgr,
):
    rep = lax.axis_index("rep")
    tp = lax.axis_index("tp")
    z = tp // NY
    y = tp % NY
    x = rep // 4
    zh = (rep // 2) % 2
    c = rep % 2
    odd = z % 2
    own_b = odd
    pair_b = 1 - odd

    def rep_of(xx, hh, cc):
        return (xx * 2 + hh) * 2 + cc

    def zdev(step):
        zz = (zh * NZ + z + step + 2 * NZ) % (2 * NZ)
        return (rep_of(x, zz // NZ, c), zz % NZ * NY + y)

    y_dev = ((rep, z * NY + (y + 1) % NY), (rep, z * NY + (y + 3) % NY))
    x_dev = ((rep_of((x + 1) % NX, zh, c), tp), (rep_of((x + 3) % NX, zh, c), tp))
    z_dev = (zdev(1), zdev(-1))
    core_dev = (rep_of(x, zh, 1 - c), tp)
    token_dev = zdev(1 - 2 * odd)
    weight_dev = zdev(2 * odd - 1)
    swap_dev = (rep, (3 - z) * NY + y)

    smalls = (
        pltpu.make_async_copy(res_hbm, res, loc.at[0]),
        pltpu.make_async_copy(own_hbm, own_ref, loc.at[1]),
        pltpu.make_async_copy(id_hbm, id_ref, loc.at[2]),
        pltpu.make_async_copy(ml_hbm, ml_ref, loc.at[3]),
        pltpu.make_async_copy(sl_hbm, sl_ref, loc.at[4]),
    )
    cp_wq = pltpu.make_async_copy(wq_hbm, raw1, loc.at[5])
    cp_wkv = pltpu.make_async_copy(wkv_hbm, w1.at[:, pl.ds(256, 256)], loc.at[6])
    cp_pool = pltpu.make_async_copy(pool_hbm, pool, loc.at[7])
    for cp in smalls:
        cp.start()

    barrier = pltpu.get_barrier_semaphore()

    def greet(dev):
        pl.semaphore_signal(barrier, inc=1, device_id=dev, device_id_type=MESH)

    for dev in y_dev + z_dev + (swap_dev,):
        greet(dev)
    for d in range(1, NREP):
        greet(((rep + d) % NREP, tp))
    cp_wq.start()
    cp_wkv.start()
    cp_pool.start()

    smalls[0].wait()
    xv = res[...].astype(F32)
    ms = jnp.mean(xv * xv, axis=-1, keepdims=True)
    g[own_b] = (xv * lax.rsqrt(ms + 1e-06) * gain_ref[...]).astype(BF16)
    pl.semaphore_wait(barrier, 5 + NREP - 1)

    def token_copy(b):
        return remote(g.at[b], g.at[b], ts.at[b], tr.at[b], *token_dev)

    def ysend(d, b):
        return remote(g.at[b], g.at[2 * (1 + d) + b], ys.at[d, b], yr.at[d, b], *y_dev[d])

    def yrecv(d, b):
        at = g.at[2 * (1 + d) + b]
        return remote(at, at, ys.at[d, b], yr.at[d, b], *y_dev[d])

    def yhalf(d, b):
        rows = pl.ds(d * HALF, HALF)
        return remote(
            g.at[2 * (1 + d) + b, rows], g.at[6 + b, rows], yhs.at[d, b], yhr.at[d, b], *y_dev[d]
        )

    def view(item, xx, cc, half=None):
        n = WROWS[item]
        first = (xx * 2 + cc) * n
        if half is not None:
            n = n // 2
            first = first + half * n
        rows = pl.ds(first, n)
        if item == 0:
            return w2.at[rows, pl.ds(256, 256)]
        if item == 1:
            return raw2.at[rows]
        return wall_ref.at[(z + (3, 1, 2)[item - 2]) % NZ, rows]

    def win_send(item):
        n = WROWS[item]
        src = (wkv_hbm, wq_hbm)[item].at[pl.ds((x * 2 + c) * n, n)]
        return remote(src, view(item, x, c), wis.at[item], wir.at[item], *weight_dev)

    def win_recv(item):
        at = view(item, x, c)
        return remote(at, at, wis.at[item], wir.at[item], *weight_dev)

    def wz_send(d):
        n = WROWS[2 + d]
        rows = pl.ds((x * 2 + c) * n, n)
        return remote(wo_hbm.at[rows], wall_ref.at[z, rows], zs.at[d], zr.at[d], *z_dev[d])

    def wz_recv(d):
        at = view(2 + d, x, c)
        return remote(at, at, zs.at[d], zr.at[d], *z_dev[d])

    def wz_half(d):
        at = view(2 + d, x, c, d)
        return remote(at, at, zhs.at[d], zhr.at[d], *z_dev[d])

    def wz_half_recv(d):
        at = view(4, x, c, d)
        return remote(at, at, zhs.at[d], zhr.at[d], *z_dev[d])

    def behind(d):
        return (x + (3 if d == 0 else 1)) % NX

    def x_copy(d, item, xx):
        at = view(item, xx, c)
        return remote(at, at, xs.at[d, item], xr.at[d, item], *x_dev[d])

    def x_half(d, item, xx):
        at = view(item, xx, c, d)
        return remote(at, at, xhs.at[d, item], xhr.at[d, item], *x_dev[d])

    def core_copy(n, item, cc):
        if n == 0:
            at = view(item, x, cc)
        elif n < 3:
            at = view(item, behind(n - 1), cc)
        else:
            at = view(item, (x + 2) % NX, cc, n - 3)
        return remote(at, at, cs.at[n, item], cr.at[n, item], *core_dev)

    def spread(item):
        for d in range(2):
            x_copy(d, item, x).start()
        core_copy(0, item, c).start()

    def spread_on(item):
        for d in range(2):
            x_copy(d, item, behind(d)).wait_recv()
            x_half(d, item, behind(d)).start()
            core_copy(1 + d, item, c).start()

    def spread_last(item):
        for d in range(2):
            x_half(d, item, (x + 2) % NX).wait_recv()
            core_copy(3 + d, item, c).start()

    def spread_done(item):
        for n in range(5):
            core_copy(n, item, 1 - c).wait_recv()

    def rq_send(d):
        to = (rep + d) % NREP
        return remote(treq.at[to], rreq.at[rep], rqs.at[d], rqr.at[d], to, tp)

    def rq_recv(d):
        frm = (rep + NREP - d) % NREP
        return remote(treq.at[frm], rreq.at[frm], rqs.at[d], rqr.at[d], frm, tp)

    def pg_send(d):
        to = (rep + d) % NREP
        return remote(sbuf.at[to], pages_ref.at[rep], pgs.at[d], pgr.at[d], to, tp)

    def pg_recv(d):
        frm = (rep + NREP - d) % NREP
        return remote(sbuf.at[frm], pages_ref.at[frm], pgs.at[d], pgr.at[d], frm, tp)

    def each(n0, n1, f):
        def body(i, carry):
            f(i)
            return carry

        lax.fori_loop(n0, n1, body, 0)

    for d in range(2):
        ysend(d, own_b).start()
    token_copy(own_b).start()
    win_send(0).start()
    win_send(1).start()

    o_iota = lax.broadcasted_iota(I32, (NREP, NB), 0)
    b_iota = lax.broadcasted_iota(I32, (1, NB), 1)
    b_up = lax.broadcasted_iota(I32, (NB, NB), 0)
    b_across = lax.broadcasted_iota(I32, (NB, NB), 1)
    for cp in smalls[1:]:
        cp.wait()
    owners = []
    columns = []
    for r in range(REQ):
        live = b_iota * BLK < ml_ref[0, r]
        owners.append(jnp.where(live, own_ref[0, r : r + 1, :], -1))
        columns.append(
            jnp.sum(jnp.where(b_up == b_across, owners[r], 0), axis=1, keepdims=True)
        )
    wanted = [jnp.zeros((NREP, NB), I32) for _ in range(CAP)]
    for r in range(REQ):
        same = (columns[r] == owners[r]) & (b_up < b_across)
        count = jnp.where(same, 1, 0)
        for e in range(r):
            count = count + jnp.where(columns[e] == owners[r], 1, 0)
        rank = jnp.sum(count, axis=0, keepdims=True)
        for s in range(CAP):
            hit = (owners[r] == o_iota) & (rank == s)
            wanted[s] = wanted[s] + jnp.where(hit, id_ref[0, r : r + 1, :], 0)
    slot_iota = lax.broadcasted_iota(I32, (NREP, 128), 1)
    table = jnp.zeros((NREP, 128), I32)
    for s in range(CAP):
        table = table + jnp.where(
            slot_iota == s, jnp.sum(wanted[s], axis=1, keepdims=True), 0
        )
    treq[...] = jnp.broadcast_to(table[:, None, :], (NREP, 8, 128))
    rreq[rep] = treq[rep]
    each(1, NREP, lambda d: rq_send(d).start())

    e0 = sl_ref[0, 0]
    e1 = e0 + sl_ref[0, 1]
    e2 = e1 + sl_ref[0, 2]

    def tables(i):
        tok = i * 128 + lax.broadcasted_iota(I32, (128, HD), 0)
        off = jnp.where(tok >= e0, ml_ref[0, 1] - e0, ml_ref[0, 0])
        off = jnp.where(tok >= e1, ml_ref[0, 2] - e1, off)
        off = jnp.where(tok >= e2, ml_ref[0, 3] - e2, off)
        lane = lax.broadcasted_iota(I32, (128, HD), 1)
        low = lane < HD // 2
        freq = jnp.exp(
            jnp.where(low, lane, lane - HD // 2).astype(F32) * (-2.0 * math.log(10000.0) / HD)
        )
        angle = (tok + off).astype(F32) * freq
        rows = pl.ds(pl.multiple_of(i * 128, 128), 128)
        ctab[rows, :] = jnp.cos(angle)
        sine = jnp.sin(angle)
        stab[rows, :] = jnp.where(low, -sine, sine)

    each(0, SUF // 128, tables)

    def split(src, dst, i):
        rows = pl.ds(pl.multiple_of(i * 1024, 1024), 1024)
        tmp[0:1024, :] = src[rows, :].astype(F32)
        to = pl.ds(pl.multiple_of(i * 512, 512), 512)
        dst[to, 0:128] = tmp[pl.ds(0, 512, stride=2), :].astype(BF16)
        dst[to, 128:256] = tmp[pl.ds(1, 512, stride=2), :].astype(BF16)

    def token_row(zz, yy):
        return pl.ds(pl.multiple_of((zz * NY + yy) * TOK, TOK), TOK)

    columns_of = (y, (y + 3) % NY, (y + 1) % NY, (y + 2) % NY)

    def swap(slot):
        zz = (3 - z) // 2 * 2 + slot % 2
        return remote(
            ex.at[slot], exr.at[slot], es.at[slot], er.at[slot], *swap_dev
        ), token_row(zz, columns_of[slot // 2])

    def project(first, count):
        rows = g[first : first + count].reshape(count * TOK, D)
        for which in (1, 0):
            out = jnp.dot(rows, (w1, w2)[which][...], preferred_element_type=F32)
            for i in range(count):
                slot = first + i
                at = token_row(z // 2 * 2 + slot % 2, columns_of[slot // 2])
                cosine = ctab[at, :]
                sine = stab[at, :]
                part = out[i * TOK : (i + 1) * TOK]
                for h in range(4):
                    vals = part[:, h * HD : (h + 1) * HD]
                    if h < 3:
                        vals = vals * cosine + pltpu.roll(vals, HD // 2, 1) * sine
                    if which == 0:
                        qkv_ref[at, h * HD : (h + 1) * HD] = vals.astype(BF16)
                    else:
                        ex[slot, :, h * HD : (h + 1) * HD] = vals.astype(BF16)
                if which == 1:
                    swap(slot)[0].start()

    def ystep(b):
        for d in range(2):
            yrecv(d, b).wait_recv()
            yhalf(d, b).start()

    token_copy(pair_b).wait_recv()
    for d in range(2):
        ysend(d, pair_b).start()
    for d in range(2):
        wz_send(d).start()
    for item in range(2):
        win_recv(item).wait_recv()
        spread(item)

    each(1, NREP, lambda d: rq_recv(d).wait_recv())
    cp_req = pltpu.make_async_copy(rreq, sreq, loc.at[8])
    cp_req.start()
    cp_req.wait()
    cp_pool.wait()

    def fill(d):
        to = (rep + d) % NREP
        for s in range(CAP):
            sbuf[to, pl.ds(s * BLK, BLK), :] = pool[jnp.clip(sreq[to, 0, s], 0, POOL - 1)]

        @pl.when(d > 0)
        def _():
            pg_send(d).start()

    each(0, NREP, fill)
    cp_page = pltpu.make_async_copy(sbuf.at[rep], pages_ref.at[rep], loc.at[9])
    cp_page.start()

    ystep(own_b)
    for d in range(2):
        wz_recv(d).wait_recv()
        wz_half(d).start()
    spread_on(0)
    spread_on(1)
    for item in (2, 3):
        spread(item)
    ystep(pair_b)
    for d in range(2):
        wz_half_recv(d).wait_recv()
    spread(4)
    cp_wq.wait()
    each(0, 9, functools.partial(split, raw1, w1))
    cp_wkv.wait()
    spread_last(0)
    spread_last(1)
    for item in (2, 3):
        spread_on(item)
    spread_done(1)
    each(0, 9, functools.partial(split, raw2, w2))
    spread_done(0)
    spread_on(4)
    project(0, 6)
    for item in (2, 3, 4):
        spread_last(item)
    for b in range(2):
        for d in range(2):
            at = g.at[6 + b, pl.ds(d * HALF, HALF)]
            remote(at, at, yhs.at[d, b], yhr.at[d, b], *y_dev[d]).wait_recv()
    project(6, 2)

    for slot in range(2 * NY):
        copy, at = swap(slot)
        copy.wait_recv()
        qkv_ref[at, :] = exr[slot]

    cp_page.wait()
    each(1, NREP, lambda d: pg_recv(d).wait_recv())
    for item in (2, 3, 4):
        spread_done(item)
    each(1, NREP, lambda d: rq_send(d).wait_send())
    each(1, NREP, lambda d: pg_send(d).wait_send())
    token_copy(own_b).wait_send()
    for d in range(2):
        win_send(d).wait_send()
        wz_send(d).wait_send()
        wz_half(d).wait_send()
        for b in range(2):
            ysend(d, b).wait_send()
            yhalf(d, b).wait_send()
        for item in range(5):
            x_copy(d, item, x).wait_send()
            x_half(d, item, behind(d)).wait_send()
    for item in range(5):
        for n in range(5):
            core_copy(n, item, c).wait_send()
    for slot in range(2 * NY):
        swap(slot)[0].wait_send()


def attend_kernel(
    qkv_ref, pages_ref, own_ref, ml_ref, sl_ref, o_ref, kpre, vpre, vsuf, acc, cnt
):
    rows_blk = 128
    keys_blk = 256
    scale = 1.0 / 600.0
    power = 50.0 / math.log(2.0)
    vsuf[:, :HD] = qkv_ref[:, 3 * HD :]
    vsuf[:, HD:] = jnp.ones((SUF, HD), BF16)
    vpre[:, HD:] = jnp.ones((REQ * NB * BLK, HD), BF16)
    for o in range(NREP):
        cnt[o] = 0
    for r in range(REQ):
        blocks = (ml_ref[0, r] + BLK - 1) // BLK
        padded = (ml_ref[0, r] + keys_blk - 1) // keys_blk * (keys_blk // BLK)

        def place(b, carry):
            o = own_ref[0, r, b]
            s = cnt[o]
            cnt[o] = s + 1
            page = pages_ref[o, pl.ds(pl.multiple_of(s * BLK, BLK), BLK), :]
            at = pl.ds(pl.multiple_of(r * NB * BLK + b * BLK, BLK), BLK)
            kpre[at, :] = page[:, :HD]
            vpre[at, :HD] = page[:, HD:]
            return carry

        def clear(b, carry):
            at = pl.ds(pl.multiple_of(r * NB * BLK + b * BLK, BLK), BLK)
            kpre[at, :] = jnp.zeros((BLK, HD), BF16)
            vpre[at, :HD] = jnp.zeros((BLK, HD), BF16)
            return carry

        lax.fori_loop(0, blocks, place, 0)
        lax.fori_loop(blocks, padded, clear, 0)

    starts = [0]
    for r in range(REQ):
        starts.append(starts[-1] + sl_ref[0, r])

    def weigh(q2, keys):
        scores = lax.dot_general(q2, keys, (((1,), (1,)), ((), ())), preferred_element_type=F32)
        return jnp.exp2(jnp.tanh(scores * scale) * power)

    def block(i, carry):
        t0 = i * rows_blk
        at = pl.ds(pl.multiple_of(t0, rows_blk), rows_blk)
        q2 = jnp.concatenate([qkv_ref[at, :HD], qkv_ref[at, HD : 2 * HD]], axis=0)
        row = lax.broadcasted_iota(I32, (2 * rows_blk, 1), 0)
        tok = t0 + jnp.where(row >= rows_blk, row - rows_blk, row)
        lane = lax.broadcasted_iota(I32, (2 * rows_blk, keys_blk), 1)
        acc[...] = jnp.zeros_like(acc)
        first = 0
        row_start = jnp.zeros_like(tok)
        for r in range(1, REQ):
            first = jnp.where(t0 >= starts[r], starts[r], first)
            row_start = jnp.where(tok >= starts[r], starts[r], row_start)
        for r in range(REQ):

            @pl.when((starts[r] < t0 + rows_blk) & (starts[r + 1] > t0))
            def _():
                limit = jnp.where((tok >= starts[r]) & (tok < starts[r + 1]), ml_ref[0, r], 0)

                def chunk(ch, inner_carry):
                    keys = pl.ds(
                        pl.multiple_of(r * NB * BLK + ch * keys_blk, keys_blk), keys_blk
                    )
                    w = weigh(q2, kpre[keys, :])
                    w = jnp.where(lane < limit - ch * keys_blk, w, 0.0).astype(BF16)
                    acc[...] += jnp.dot(w, vpre[keys, :], preferred_element_type=F32)
                    return inner_carry

                lax.fori_loop(0, (ml_ref[0, r] + keys_blk - 1) // keys_blk, chunk, 0)

        def own_chunk(ch, inner_carry):
            keys = pl.ds(pl.multiple_of(ch * keys_blk, keys_blk), keys_blk)
            w = weigh(q2, qkv_ref[keys, 2 * HD : 3 * HD])
            key = lane + ch * keys_blk
            w = jnp.where((key >= row_start) & (key <= tok), w, 0.0).astype(BF16)
            acc[...] += jnp.dot(w, vsuf[keys, :], preferred_element_type=F32)
            return inner_carry

        lax.fori_loop(first // keys_blk, (t0 + rows_blk - 1) // keys_blk + 1, own_chunk, 0)
        done = (acc[:, :HD] / acc[:, HD:]).astype(BF16)
        o_ref[at, :HD] = done[:rows_blk]
        o_ref[at, HD:] = done[rows_blk:]
        return carry

    lax.fori_loop(0, SUF // rows_blk, block, 0)


def output_kernel(
    att_ref,
    wo_hbm,
    wall_hbm,
    res_ref,
    gain_ref,
    out_ref,
    a,
    w,
    p,
    rel,
    sb,
    rx,
    br,
    loc,
    asm,
    arm,
    hs,
    hr,
    os,
    orr,
    ss,
    sr,
):
    rep = lax.axis_index("rep")
    tp = lax.axis_index("tp")
    z = tp // NY
    y = tp % NY
    rows = NY * TOK
    yn = (z * NY + (y + 1) % NY, z * NY + (y + 3) % NY)

    def wload(d):
        zz = (z + d) % NZ
        src = wo_hbm if d == 0 else wall_hbm.at[zz]
        return pltpu.make_async_copy(src, w.at[d], loc.at[d])

    for d in range(NZ):
        wload(d).start()

    barrier = pltpu.get_barrier_semaphore()
    for d in range(1, NZ):
        pl.semaphore_signal(
            barrier, inc=1, device_id=(rep, (z + d) % NZ * NY + y), device_id_type=MESH
        )
    for d in range(2):
        pl.semaphore_signal(barrier, inc=1, device_id=(rep, yn[d]), device_id_type=MESH)
    pl.semaphore_wait(barrier, NZ - 1 + 2)

    def asend(d):
        to = (z + d) % NZ
        return remote(
            att_ref.at[pl.ds(to * rows, rows)], a.at[NZ - d], asm.at[d], arm.at[NZ - d], rep,
            to * NY + y,
        )

    def arecv(d):
        return remote(a.at[d], a.at[d], asm.at[d], arm.at[d], rep, yn[0])

    for d in range(1, NZ):
        asend(d).start()
    a[0] = att_ref[pl.ds(pl.multiple_of(z * rows, rows), rows), :]
    for d in range(NZ):
        wload(d).wait()
    for d in range(1, NZ):
        arecv(d).wait_recv()

    up = ((y + 1) % NY, (y + 3) % NY)
    far = (y + 2) % NY

    def via(d, n):
        at = pl.ds(d * HALF, HALF)
        return remote(p.at[n, far, at], rel.at[d, n], hs.at[d, n], hr.at[d, n], rep, yn[d])

    def straight(d, n):
        at = pl.ds((1 - d) * HALF, HALF)
        return remote(p.at[n, up[d], at], rx.at[d, n, at], os.at[d, n], orr.at[d, n], rep, yn[d])

    def summed(d, n):
        at = pl.ds(d * HALF, HALF)
        return remote(sb.at[d, n], rx.at[d, n, at], ss.at[d, n], sr.at[d, n], rep, yn[d])

    for n in range(NC):
        total = jnp.dot(a[0], w[0, :, n * CW : (n + 1) * CW], preferred_element_type=F32)
        for d in range(1, NZ):
            total += jnp.dot(a[d], w[d, :, n * CW : (n + 1) * CW], preferred_element_type=F32)
        p[n] = total.astype(BF16).reshape(NY, TOK, CW)
        for d in range(2):
            via(d, n).start()
        for d in range(2):
            straight(d, n).start()
    for n in range(NC):
        for d in range(2):
            via(d, n).wait_recv()
            at = pl.ds(d * HALF, HALF)
            sb[d, n] = (p[n, up[d], at].astype(F32) + rel[d, n].astype(F32)).astype(BF16)
            summed(d, n).start()
    square = jnp.zeros((TOK, 1), F32)
    for n in range(NC):
        for d in range(2):
            straight(d, n).wait_recv()
            summed(d, n).wait_recv()
        total = p[n, y].astype(F32) + rx[0, n].astype(F32) + rx[1, n].astype(F32)
        br[n] = total
        square += jnp.sum(total * total, axis=-1, keepdims=True)
    inv = lax.rsqrt(square * (1.0 / D) + 1e-06)
    for n in range(NC):
        at = slice(n * CW, (n + 1) * CW)
        out_ref[:, at] = (
            res_ref[:, at].astype(F32) + br[n] * inv * gain_ref[:, at]
        ).astype(BF16)
    for d in range(1, NZ):
        asend(d).wait_send()
    for n in range(NC):
        for d in range(2):
            via(d, n).wait_send()
            straight(d, n).wait_send()
            summed(d, n).wait_send()


VM = pl.BlockSpec(memory_space=pltpu.VMEM)
SM = pl.BlockSpec(memory_space=pltpu.SMEM)
ANY = pl.BlockSpec(memory_space=pl.ANY)


def dma(*shape):
    return pltpu.SemaphoreType.DMA(shape)


def per_device(
    residual_in,
    attn_gain,
    branch_gain,
    w_query,
    w_keyval,
    w_out,
    page_pool,
    match_len,
    block_owner,
    block_id,
    suffix_len,
):
    wq = w_query.reshape(2 * D, HD)
    wkv = w_keyval.reshape(D, 2 * HD)
    wo = w_out.reshape(2 * HD, D)
    pool = page_pool.reshape(POOL, BLK, 2 * HD)
    qkv, pages, wall = pl.pallas_call(
        gather_kernel,
        out_shape=(
            jax.ShapeDtypeStruct((SUF, 4 * HD), BF16),
            jax.ShapeDtypeStruct((NREP, CAP * BLK, 2 * HD), BF16),
            jax.ShapeDtypeStruct((NZ, 2 * HD, D), BF16),
        ),
        in_specs=[ANY, VM] + [ANY] * 8,
        out_specs=(VM, ANY, ANY),
        scratch_shapes=[
            pltpu.VMEM((TOK, D), BF16),
            pltpu.VMEM((POOL, BLK, 2 * HD), BF16),
            pltpu.VMEM((1, REQ, NB), I32),
            pltpu.VMEM((1, REQ, NB), I32),
            pltpu.SMEM((1, REQ), I32),
            pltpu.SMEM((1, REQ), I32),
            pltpu.VMEM((2 * NY, TOK, D), BF16),
            pltpu.VMEM((2 * D, HD), BF16),
            pltpu.VMEM((2 * D, HD), BF16),
            pltpu.VMEM((D, 4 * HD), BF16),
            pltpu.VMEM((D, 4 * HD), BF16),
            pltpu.VMEM((1032, HD), F32),
            pltpu.VMEM((SUF, HD), F32),
            pltpu.VMEM((SUF, HD), F32),
            pltpu.VMEM((2 * NY, TOK, 4 * HD), BF16),
            pltpu.VMEM((2 * NY, TOK, 4 * HD), BF16),
            pltpu.VMEM((NREP, 8, 128), I32),
            pltpu.VMEM((NREP, 8, 128), I32),
            pltpu.SMEM((NREP, 8, 128), I32),
            pltpu.VMEM((NREP, CAP * BLK, 2 * HD), BF16),
            dma(10),
            dma(2),
            dma(2),
            dma(2, 2),
            dma(2, 2),
            dma(2, 2),
            dma(2, 2),
            dma(2),
            dma(2),
            dma(2),
            dma(2),
            dma(2),
            dma(2),
            dma(2, 5),
            dma(2, 5),
            dma(2, 5),
            dma(2, 5),
            dma(5, 5),
            dma(5, 5),
            dma(2 * NY),
            dma(2 * NY),
            dma(NREP),
            dma(NREP),
            dma(NREP),
            dma(NREP),
        ],
        compiler_params=pltpu.CompilerParams(
            collective_id=0, has_side_effects=True, vmem_limit_bytes=60 << 20
        ),
        name="gather_project",
    )(
        residual_in,
        attn_gain.reshape(1, D),
        wq,
        wkv,
        wo,
        pool,
        block_owner,
        block_id,
        match_len,
        suffix_len,
    )
    attended = pl.pallas_call(
        attend_kernel,
        out_shape=jax.ShapeDtypeStruct((SUF, 2 * HD), BF16),
        in_specs=[VM, VM, SM, SM, SM],
        out_specs=VM,
        scratch_shapes=[
            pltpu.VMEM((REQ * NB * BLK, HD), BF16),
            pltpu.VMEM((REQ * NB * BLK, 2 * HD), BF16),
            pltpu.VMEM((SUF, 2 * HD), BF16),
            pltpu.VMEM((256, 256), F32),
            pltpu.SMEM((NREP,), I32),
        ],
        compiler_params=pltpu.CompilerParams(vmem_limit_bytes=32 << 20),
        name="attend",
    )(qkv, pages, block_owner, match_len, suffix_len)
    return pl.pallas_call(
        output_kernel,
        out_shape=jax.ShapeDtypeStruct((TOK, D), BF16),
        in_specs=[VM, ANY, ANY, VM, VM],
        out_specs=VM,
        scratch_shapes=[
            pltpu.VMEM((NZ, NY * TOK, 2 * HD), BF16),
            pltpu.VMEM((NZ, 2 * HD, D), BF16),
            pltpu.VMEM((NC, NY, TOK, CW), BF16),
            pltpu.VMEM((2, NC, HALF, CW), BF16),
            pltpu.VMEM((2, NC, HALF, CW), BF16),
            pltpu.VMEM((2, NC, TOK, CW), BF16),
            pltpu.VMEM((NC, TOK, CW), F32),
            dma(NZ),
            dma(NZ),
            dma(NZ),
            dma(2, NC),
            dma(2, NC),
            dma(2, NC),
            dma(2, NC),
            dma(2, NC),
            dma(2, NC),
        ],
        compiler_params=pltpu.CompilerParams(
            collective_id=1, has_side_effects=True, vmem_limit_bytes=44 << 20
        ),
        name="project_out",
    )(attended, wo, wall, residual_in, branch_gain.reshape(1, D))


def solution(mesh):
    placed = (
        P(("rep", "tp"), None),
        P(),
        P(),
        P(None, "tp", None),
        P(None, "tp", None),
        P("tp", None, None),
        P("rep", None, "tp", None),
        P("rep", None),
        P("rep", None, None),
        P("rep", None, None),
        P("rep", None),
    )
    return jax.shard_map(
        per_device, mesh=mesh, in_specs=placed, out_specs=P(("rep", "tp"), None), check_vma=False
    )
```

time: 183 us -> 161 us (0.88); the launches traced: 183 us -> 159 us
  Pallas kernels: 173 us -> 154 us
  local copies, waits for them, and re-layouts: 9.78 us -> 4.8 us
    pallas_call x1, Pallas kernels: 52.3 us -> 37.8 us  [per_device(): pl.pallas_call(output_kernel, out_shape=jax.ShapeDtypeStruct((TOK, D), BF...]
    unnamed x21 -> x17, local copies, waits for them, and re-layouts: 9.02 us -> 3.44 us
    pallas_call x1, Pallas kernels: 106 us -> 104 us  [per_device(): pl.pallas_call(gather_kernel, out_shape=(jax.ShapeDtypeStruct((SUF, 4 * H...]
    pallas_call x1, Pallas kernels: 14.4 us -> 12.3 us  [per_device(): pl.pallas_call(attend_kernel, out_shape=jax.ShapeDtypeStruct((SUF, 2 * HD...]
where the time goes in v2:
time: 161 us; the launch traced here: 159 us
  Pallas kernels  154 us (96%)
  local copies, waits for them, and re-layouts  4.8 us (3%)
    pallas_call x1, Pallas kernels, per_device(): pl.pallas_call(gather_kernel, out_shape=(jax.ShapeDtypeStruct((SUF, 4 * H...  104 us
    pallas_call x1, Pallas kernels, per_device(): pl.pallas_call(output_kernel, out_shape=jax.ShapeDtypeStruct((TOK, D), BF...  37.8 us
    pallas_call x1, Pallas kernels, per_device(): pl.pallas_call(attend_kernel, out_shape=jax.ShapeDtypeStruct((SUF, 2 * HD...  12.3 us
    unnamed x17, local copies, waits for them, and re-layouts  3.44 us

profile of v2, /device:TPU:40, one launch (start us, length us, event | category | flops | bytes accessed | tf_op | source)
XLA Modules:
  0.0 158.9 jit_solution(10937803006099434321)
XLA Ops:
  0.0 1.3 reshape.18.gain_ref
  1.3 0.0 copy-start.4
  1.3 0.0 copy-start.5
  1.4 0.0 copy-start.6
  1.4 0.0 copy-start.7
  1.4 0.0 copy-start.1
  1.4 103.9 %gather_project.1 = (bf16[1024,512]{1,0:T(8,128)(2,1)}, bf16[16,128,256]{2,1,0:T(8,128)(2,1)}, bf16[4,256,4608]{2,1,0:T(8,128)(2,1)}) custom-call(bf16[64,4608]{1,0:T(8,128)(2,1)} %res_ref.1, f32[1,4608]{1,0:T(1,128)} %reshape.18.gain_ref, bf16[9216,128]{1,0:T(8,128)(2,1)} %bitcast.6, bf16[4608,256]{1,0:T(8,128)(2,1)} %bitcast.7, bf16[256,4608]{1,0:T(8,128)(2,1)} %bitcast.4, ...), custom_call_target="tpu_custom_call" | custom-call | tf_op jit(solution)/shard_map/gather_project/pallas_call | solution.py:712
  105.3 0.0 copy-start
  105.3 0.0 copy-done.4
  105.3 0.0 copy-done.5
  105.3 0.0 copy-done.6
  105.3 0.0 copy-start.2
  105.3 1.4 copy-done.2
  106.7 0.0 copy-start.3
  106.7 1.2 copy-done.3
  107.9 12.3 %attend.1.att_ref = bf16[1024,256]{1,0:T(8,128)(2,1)S(1)} custom-call(bf16[1024,512]{1,0:T(8,128)(2,1)S(1)} %copy-done.2, bf16[16,128,256]{2,1,0:T(8,128)(2,1)S(1)} %copy-done.3, s32[1,4,32]{2,1,0:T(4,128)S(1)} %copy-done.4, s32[1,4]{1,0:T(1,128)S(1)} %copy-done.5, s32[1,4]{1,0:T(1,128)S(1)} %copy-done.6), custom_call_target="tpu_custom_call" | custom-call | tf_op jit(solution)/shard_map/attend/pallas_call | solution.py:784
  120.2 0.0 copy-done.7
  120.2 0.0 copy-done.1
  120.2 0.0 copy-done
  120.3 37.8 %project_out.1 = bf16[64,4608]{1,0:T(8,128)(2,1)S(1)} custom-call(bf16[1024,256]{1,0:T(8,128)(2,1)S(1)} %attend.1.att_ref, bf16[256,4608]{1,0:T(8,128)(2,1)S(1)} %bitcast.5, bf16[4,256,4608]{2,1,0:T(8,128)(2,1)} %get-tuple-element.10.wall_hbm, bf16[64,4608]{1,0:T(8,128)(2,1)S(1)} %copy-done.1, f32[1,4608]{1,0:T(1,128)S(1)} %reshape.23.gain_ref), custom_call_target="tpu_custom_call" | custom-call | tf_op jit(solution)/shard_map/project_out/pallas_call | solution.py:799
  158.1 0.8 copy.13
  (1 shorter events, 0.0 us)
Async XLA Ops:
  1.3 103.9 %copy-start.4 = (s32[1,4,32]{2,1,0:T(4,128)S(1)}, s32[1,4,32]{2,1,0:T(4,128)}, u32[]{:S(2)}) copy-start(s32[1,4,32]{2,1,0:T(4,128)} %own_ref.1) | copy-start | bytes 1540
  1.3 103.9 %copy-start.5 = (s32[1,4]{1,0:T(1,128)S(1)}, s32[1,4]{1,0:T(1,128)}, u32[]{:S(2)}) copy-start(s32[1,4]{1,0:T(1,128)} %ml_ref.1) | copy-start | bytes 52
  1.4 103.9 %copy-start.6 = (s32[1,4]{1,0:T(1,128)S(1)}, s32[1,4]{1,0:T(1,128)}, u32[]{:S(2)}) copy-start(s32[1,4]{1,0:T(1,128)} %sl_ref.1) | copy-start | bytes 52
  1.4 118.9 %copy-start.7 = (f32[4608]{0:T(1024)S(1)}, f32[4608]{0:T(1024)}, u32[]{:S(2)}) copy-start(f32[4608]{0:T(1024)} %param.13) | copy-start | bytes 55300
  1.4 118.9 %copy-start.1 = (bf16[64,4608]{1,0:T(8,128)(2,1)S(1)}, bf16[64,4608]{1,0:T(8,128)(2,1)}, u32[]{:S(2)}) copy-start(bf16[64,4608]{1,0:T(8,128)(2,1)} %res_ref.1) | copy-start | bytes 1769476
  105.3 15.0 %copy-start = (bf16[2,128,4608]{2,1,0:T(8,128)(2,1)S(1)}, bf16[2,128,4608]{2,1,0:T(8,128)(2,1)}, u32[]{:S(2)}) copy-start(bf16[2,128,4608]{2,1,0:T(8,128)(2,1)} %param.16) | copy-start | bytes 7077892
  105.3 1.4 copy-start.2
  106.7 1.2 copy-start.3

commit v3 on v2

--- a/solution.py
+++ b/solution.py
@@ -45,7 +45,7 @@
 
 def gather_kernel(
     res_hbm,
-    gain_ref,
+    gain_hbm,
     wq_hbm,
     wkv_hbm,
     wo_hbm,
@@ -58,6 +58,7 @@
     pages_ref,
     wall_ref,
     res,
+    gain_ref,
     pool,
     own_ref,
     id_ref,
@@ -135,6 +136,7 @@
         pltpu.make_async_copy(id_hbm, id_ref, loc.at[2]),
         pltpu.make_async_copy(ml_hbm, ml_ref, loc.at[3]),
         pltpu.make_async_copy(sl_hbm, sl_ref, loc.at[4]),
+        pltpu.make_async_copy(gain_hbm, gain_ref, loc.at[10]),
     )
     cp_wq = pltpu.make_async_copy(wq_hbm, raw1, loc.at[5])
     cp_wkv = pltpu.make_async_copy(wkv_hbm, w1.at[:, pl.ds(256, 256)], loc.at[6])
@@ -156,9 +158,10 @@
     cp_pool.start()
 
     smalls[0].wait()
+    smalls[5].wait()
     xv = res[...].astype(F32)
     ms = jnp.mean(xv * xv, axis=-1, keepdims=True)
-    g[own_b] = (xv * lax.rsqrt(ms + 1e-06) * gain_ref[...]).astype(BF16)
+    g[own_b] = (xv * lax.rsqrt(ms + 1e-06) * gain_ref[...].reshape(1, D)).astype(BF16)
     pl.semaphore_wait(barrier, 5 + NREP - 1)
 
     def token_copy(b):
@@ -256,21 +259,25 @@
         for n in range(5):
             core_copy(n, item, 1 - c).wait_recv()
 
-    def rq_send(d):
-        to = (rep + d) % NREP
-        return remote(treq.at[to], rreq.at[rep], rqs.at[d], rqr.at[d], to, tp)
-
-    def rq_recv(d):
-        frm = (rep + NREP - d) % NREP
-        return remote(treq.at[frm], rreq.at[frm], rqs.at[d], rqr.at[d], frm, tp)
-
-    def pg_send(d):
-        to = (rep + d) % NREP
-        return remote(sbuf.at[to], pages_ref.at[rep], pgs.at[d], pgr.at[d], to, tp)
-
-    def pg_recv(d):
-        frm = (rep + NREP - d) % NREP
-        return remote(sbuf.at[frm], pages_ref.at[frm], pgs.at[d], pgr.at[d], frm, tp)
+    def to_of(k):
+        return rep_of((x + k // 4) % NX, (zh + k // 2 % 2) % 2, (c + k % 2) % 2)
+
+    def from_of(k):
+        return rep_of((x + NX - k // 4) % NX, (zh + k // 2 % 2) % 2, (c + k % 2) % 2)
+
+    def rq_send(k):
+        return remote(treq.at[to_of(k)], rreq.at[rep], rqs.at[k], rqr.at[k], to_of(k), tp)
+
+    def rq_recv(k):
+        at = rreq.at[from_of(k)]
+        return remote(at, at, rqs.at[k], rqr.at[k], from_of(k), tp)
+
+    def pg_send(k):
+        return remote(sbuf.at[to_of(k)], pages_ref.at[rep], pgs.at[k], pgr.at[k], to_of(k), tp)
+
+    def pg_recv(k):
+        at = pages_ref.at[from_of(k)]
+        return remote(at, at, pgs.at[k], pgr.at[k], from_of(k), tp)
 
     def each(n0, n1, f):
         def body(i, carry):
@@ -289,7 +296,7 @@
     b_iota = lax.broadcasted_iota(I32, (1, NB), 1)
     b_up = lax.broadcasted_iota(I32, (NB, NB), 0)
     b_across = lax.broadcasted_iota(I32, (NB, NB), 1)
-    for cp in smalls[1:]:
+    for cp in smalls[1:5]:
         cp.wait()
     owners = []
     columns = []
@@ -319,6 +326,26 @@
     rreq[rep] = treq[rep]
     each(1, NREP, lambda d: rq_send(d).start())
 
+    each(1, NREP, lambda d: rq_recv(d).wait_recv())
+    cp_req = pltpu.make_async_copy(rreq, sreq, loc.at[8])
+    cp_req.start()
+    cp_req.wait()
+    cp_pool.wait()
+
+    def fill(half, i):
+        k = i // 2 * 4 + i % 2 + 2 * half
+        to = to_of(k)
+        for s in range(CAP):
+            sbuf[to, pl.ds(s * BLK, BLK), :] = pool[jnp.clip(sreq[to, 0, s], 0, POOL - 1)]
+
+        @pl.when(k > 0)
+        def _():
+            pg_send(k).start()
+
+    each(0, 8, functools.partial(fill, 0))
+    cp_page = pltpu.make_async_copy(sbuf.at[rep], pages_ref.at[rep], loc.at[9])
+    cp_page.start()
+
     e0 = sl_ref[0, 0]
     e1 = e0 + sl_ref[0, 1]
     e2 = e1 + sl_ref[0, 2]
@@ -385,65 +412,47 @@
             yrecv(d, b).wait_recv()
             yhalf(d, b).start()
 
+    cp_wq.wait()
+    each(0, 9, functools.partial(split, raw1, w1))
     token_copy(pair_b).wait_recv()
     for d in range(2):
         ysend(d, pair_b).start()
-    for d in range(2):
-        wz_send(d).start()
     for item in range(2):
         win_recv(item).wait_recv()
         spread(item)
-
-    each(1, NREP, lambda d: rq_recv(d).wait_recv())
-    cp_req = pltpu.make_async_copy(rreq, sreq, loc.at[8])
-    cp_req.start()
-    cp_req.wait()
-    cp_pool.wait()
-
-    def fill(d):
-        to = (rep + d) % NREP
-        for s in range(CAP):
-            sbuf[to, pl.ds(s * BLK, BLK), :] = pool[jnp.clip(sreq[to, 0, s], 0, POOL - 1)]
-
-        @pl.when(d > 0)
-        def _():
-            pg_send(d).start()
-
-    each(0, NREP, fill)
-    cp_page = pltpu.make_async_copy(sbuf.at[rep], pages_ref.at[rep], loc.at[9])
-    cp_page.start()
-
+    for d in range(2):
+        wz_send(d).start()
+    each(0, 8, functools.partial(fill, 1))
     ystep(own_b)
+    spread_on(0)
+    spread_on(1)
     for d in range(2):
         wz_recv(d).wait_recv()
         wz_half(d).start()
-    spread_on(0)
-    spread_on(1)
+    spread_last(0)
+    spread_last(1)
     for item in (2, 3):
         spread(item)
+    cp_wkv.wait()
+    spread_done(1)
+    each(0, 9, functools.partial(split, raw2, w2))
+    spread_done(0)
+    project(0, 2)
     ystep(pair_b)
     for d in range(2):
         wz_half_recv(d).wait_recv()
     spread(4)
-    cp_wq.wait()
-    each(0, 9, functools.partial(split, raw1, w1))
-    cp_wkv.wait()
-    spread_last(0)
-    spread_last(1)
+    project(2, 4)
     for item in (2, 3):
         spread_on(item)
-    spread_done(1)
-    each(0, 9, functools.partial(split, raw2, w2))
-    spread_done(0)
-    spread_on(4)
-    project(0, 6)
-    for item in (2, 3, 4):
-        spread_last(item)
     for b in range(2):
         for d in range(2):
             at = g.at[6 + b, pl.ds(d * HALF, HALF)]
             remote(at, at, yhs.at[d, b], yhr.at[d, b], *y_dev[d]).wait_recv()
     project(6, 2)
+    spread_on(4)
+    for item in (2, 3, 4):
+        spread_last(item)
 
     for slot in range(2 * NY):
         copy, at = swap(slot)
@@ -568,9 +577,11 @@
     att_ref,
     wo_hbm,
     wall_hbm,
-    res_ref,
+    res_hbm,
+    gain_hbm,
+    out_ref,
+    res,
     gain_ref,
-    out_ref,
     a,
     w,
     p,
@@ -592,16 +603,19 @@
     tp = lax.axis_index("tp")
     z = tp // NY
     y = tp % NY
-    rows = NY * TOK
-    yn = (z * NY + (y + 1) % NY, z * NY + (y + 3) % NY)
+    y_dev = (z * NY + (y + 1) % NY, z * NY + (y + 3) % NY)
+    group_col = ((y + 2) % NY, (y + 1) % NY, (y + 3) % NY, y)
 
     def wload(d):
-        zz = (z + d) % NZ
-        src = wo_hbm if d == 0 else wall_hbm.at[zz]
-        return pltpu.make_async_copy(src, w.at[d], loc.at[d])
-
+        src = wo_hbm if d == 0 else wall_hbm.at[(z + d) % NZ]
+        return pltpu.make_async_copy(src, w.at[pl.ds(d * 256, 256)], loc.at[d])
+
+    cp_res = pltpu.make_async_copy(res_hbm, res, loc.at[NZ])
     for d in range(NZ):
         wload(d).start()
+    cp_gain = pltpu.make_async_copy(gain_hbm, gain_ref, loc.at[NZ + 1])
+    cp_res.start()
+    cp_gain.start()
 
     barrier = pltpu.get_barrier_semaphore()
     for d in range(1, NZ):
@@ -609,73 +623,94 @@
             barrier, inc=1, device_id=(rep, (z + d) % NZ * NY + y), device_id_type=MESH
         )
     for d in range(2):
-        pl.semaphore_signal(barrier, inc=1, device_id=(rep, yn[d]), device_id_type=MESH)
+        pl.semaphore_signal(barrier, inc=1, device_id=(rep, y_dev[d]), device_id_type=MESH)
+    for i in range(NY):
+        at = pl.ds(pl.multiple_of((z * NY + group_col[i]) * TOK, TOK), TOK)
+        a[i * TOK : (i + 1) * TOK, 0:256] = att_ref[at, :]
     pl.semaphore_wait(barrier, NZ - 1 + 2)
 
-    def asend(d):
+    def asend(d, i):
         to = (z + d) % NZ
+        e = NZ - d
         return remote(
-            att_ref.at[pl.ds(to * rows, rows)], a.at[NZ - d], asm.at[d], arm.at[NZ - d], rep,
+            att_ref.at[pl.ds((to * NY + group_col[i]) * TOK, TOK)],
+            a.at[pl.ds(i * TOK, TOK), pl.ds(e * 256, 256)],
+            asm.at[e, i],
+            arm.at[e, i],
+            rep,
             to * NY + y,
         )
 
-    def arecv(d):
-        return remote(a.at[d], a.at[d], asm.at[d], arm.at[d], rep, yn[0])
-
-    for d in range(1, NZ):
-        asend(d).start()
-    a[0] = att_ref[pl.ds(pl.multiple_of(z * rows, rows), rows), :]
+    def arecv(e, i):
+        at = a.at[pl.ds(i * TOK, TOK), pl.ds(e * 256, 256)]
+        return remote(at, at, asm.at[e, i], arm.at[e, i], rep, y_dev[0])
+
+    for i in range(NY):
+        for d in range(1, NZ):
+            asend(d, i).start()
+
+    def via(d, n):
+        at = pl.ds(d * HALF, HALF)
+        return remote(p.at[n, 0, at], rel.at[d, n], hs.at[d, n], hr.at[d, n], rep, y_dev[d])
+
+    def straight(d, n):
+        at = pl.ds((1 - d) * HALF, HALF)
+        return remote(p.at[n, 1 + d, at], rx.at[d, n, at], os.at[d, n], orr.at[d, n], rep, y_dev[d])
+
+    def summed(d, n):
+        at = pl.ds(d * HALF, HALF)
+        return remote(sb.at[d, n], rx.at[d, n, at], ss.at[d, n], sr.at[d, n], rep, y_dev[d])
+
+    def product(first, count, n):
+        return jnp.dot(
+            a[first * TOK : (first + count) * TOK, :],
+            w[:, n * CW : (n + 1) * CW],
+            preferred_element_type=F32,
+        )
+
     for d in range(NZ):
         wload(d).wait()
-    for d in range(1, NZ):
-        arecv(d).wait_recv()
-
-    up = ((y + 1) % NY, (y + 3) % NY)
-    far = (y + 2) % NY
-
-    def via(d, n):
-        at = pl.ds(d * HALF, HALF)
-        return remote(p.at[n, far, at], rel.at[d, n], hs.at[d, n], hr.at[d, n], rep, yn[d])
-
-    def straight(d, n):
-        at = pl.ds((1 - d) * HALF, HALF)
-        return remote(p.at[n, up[d], at], rx.at[d, n, at], os.at[d, n], orr.at[d, n], rep, yn[d])
-
-    def summed(d, n):
-        at = pl.ds(d * HALF, HALF)
-        return remote(sb.at[d, n], rx.at[d, n, at], ss.at[d, n], sr.at[d, n], rep, yn[d])
-
+    for e in range(1, NZ):
+        arecv(e, 0).wait_recv()
     for n in range(NC):
-        total = jnp.dot(a[0], w[0, :, n * CW : (n + 1) * CW], preferred_element_type=F32)
-        for d in range(1, NZ):
-            total += jnp.dot(a[d], w[d, :, n * CW : (n + 1) * CW], preferred_element_type=F32)
-        p[n] = total.astype(BF16).reshape(NY, TOK, CW)
+        p[n, 0] = product(0, 1, n).astype(BF16)
         for d in range(2):
             via(d, n).start()
+    for i in (1, 2):
+        for e in range(1, NZ):
+            arecv(e, i).wait_recv()
+    for n in range(NC):
+        p[n, 1:3] = product(1, 2, n).astype(BF16).reshape(2, TOK, CW)
         for d in range(2):
             straight(d, n).start()
     for n in range(NC):
         for d in range(2):
             via(d, n).wait_recv()
             at = pl.ds(d * HALF, HALF)
-            sb[d, n] = (p[n, up[d], at].astype(F32) + rel[d, n].astype(F32)).astype(BF16)
+            sb[d, n] = (p[n, 1 + d, at].astype(F32) + rel[d, n].astype(F32)).astype(BF16)
             summed(d, n).start()
+    for e in range(1, NZ):
+        arecv(e, 3).wait_recv()
+    for n in range(NC):
+        br[n] = product(3, 1, n).astype(BF16).astype(F32)
+    cp_res.wait()
+    cp_gain.wait()
     square = jnp.zeros((TOK, 1), F32)
     for n in range(NC):
         for d in range(2):
             straight(d, n).wait_recv()
             summed(d, n).wait_recv()
-        total = p[n, y].astype(F32) + rx[0, n].astype(F32) + rx[1, n].astype(F32)
+        total = br[n] + rx[0, n].astype(F32) + rx[1, n].astype(F32)
         br[n] = total
         square += jnp.sum(total * total, axis=-1, keepdims=True)
     inv = lax.rsqrt(square * (1.0 / D) + 1e-06)
+    gain = gain_ref[...].reshape(1, D)
     for n in range(NC):
         at = slice(n * CW, (n + 1) * CW)
-        out_ref[:, at] = (
-            res_ref[:, at].astype(F32) + br[n] * inv * gain_ref[:, at]
-        ).astype(BF16)
-    for d in range(1, NZ):
-        asend(d).wait_send()
+        out_ref[:, at] = (res[:, at].astype(F32) + br[n] * inv * gain[:, at]).astype(BF16)
+    for i in range(NY):
+        for d in range(1, NZ):
+            asend(d, i).wait_send()
     for n in range(NC):
         for d in range(2):
             via(d, n).wait_send()
@@ -686,6 +721,7 @@
 VM = pl.BlockSpec(memory_space=pltpu.VMEM)
 SM = pl.BlockSpec(memory_space=pltpu.SMEM)
 ANY = pl.BlockSpec(memory_space=pl.ANY)
+HBM = pl.BlockSpec(memory_space=pltpu.HBM)
 
 
 def dma(*shape):
@@ -705,6 +741,7 @@
     block_id,
     suffix_len,
 ):
+    far = functools.partial(pltpu.with_memory_space_constraint, memory_space=pltpu.HBM)
     wq = w_query.reshape(2 * D, HD)
     wkv = w_keyval.reshape(D, 2 * HD)
     wo = w_out.reshape(2 * HD, D)
@@ -716,10 +753,11 @@
             jax.ShapeDtypeStruct((NREP, CAP * BLK, 2 * HD), BF16),
             jax.ShapeDtypeStruct((NZ, 2 * HD, D), BF16),
         ),
-        in_specs=[ANY, VM] + [ANY] * 8,
-        out_specs=(VM, ANY, ANY),
+        in_specs=[HBM] * 10,
+        out_specs=(VM, ANY, HBM),
         scratch_shapes=[
             pltpu.VMEM((TOK, D), BF16),
+            pltpu.VMEM((D,), F32),
             pltpu.VMEM((POOL, BLK, 2 * HD), BF16),
             pltpu.VMEM((1, REQ, NB), I32),
             pltpu.VMEM((1, REQ, NB), I32),
@@ -739,7 +777,7 @@
             pltpu.VMEM((NREP, 8, 128), I32),
             pltpu.SMEM((NREP, 8, 128), I32),
             pltpu.VMEM((NREP, CAP * BLK, 2 * HD), BF16),
-            dma(10),
+            dma(11),
             dma(2),
             dma(2),
             dma(2, 2),
@@ -766,20 +804,20 @@
             dma(NREP),
         ],
         compiler_params=pltpu.CompilerParams(
-            collective_id=0, has_side_effects=True, vmem_limit_bytes=60 << 20
+            collective_id=0, has_side_effects=True, vmem_limit_bytes=44 << 20
         ),
         name="gather_project",
     )(
-        residual_in,
-        attn_gain.reshape(1, D),
-        wq,
-        wkv,
-        wo,
-        pool,
-        block_owner,
-        block_id,
-        match_len,
-        suffix_len,
+        far(residual_in),
+        far(attn_gain),
+        far(wq),
+        far(wkv),
+        far(wo),
+        far(pool),
+        far(block_owner),
+        far(block_id),
+        far(match_len),
+        far(suffix_len),
     )
     attended = pl.pallas_call(
         attend_kernel,
@@ -799,19 +837,21 @@
     return pl.pallas_call(
         output_kernel,
         out_shape=jax.ShapeDtypeStruct((TOK, D), BF16),
-        in_specs=[VM, ANY, ANY, VM, VM],
+        in_specs=[VM, HBM, HBM, HBM, HBM],
         out_specs=VM,
         scratch_shapes=[
-            pltpu.VMEM((NZ, NY * TOK, 2 * HD), BF16),
-            pltpu.VMEM((NZ, 2 * HD, D), BF16),
-            pltpu.VMEM((NC, NY, TOK, CW), BF16),
+            pltpu.VMEM((TOK, D), BF16),
+            pltpu.VMEM((D,), F32),
+            pltpu.VMEM((NY * TOK, NZ * 2 * HD), BF16),
+            pltpu.VMEM((NZ * 2 * HD, D), BF16),
+            pltpu.VMEM((NC, 3, TOK, CW), BF16),
             pltpu.VMEM((2, NC, HALF, CW), BF16),
             pltpu.VMEM((2, NC, HALF, CW), BF16),
             pltpu.VMEM((2, NC, TOK, CW), BF16),
             pltpu.VMEM((NC, TOK, CW), F32),
-            dma(NZ),
-            dma(NZ),
-            dma(NZ),
+            dma(NZ + 2),
+            dma(NZ, NY),
+            dma(NZ, NY),
             dma(2, NC),
             dma(2, NC),
             dma(2, NC),
@@ -823,7 +863,7 @@
             collective_id=1, has_side_effects=True, vmem_limit_bytes=44 << 20
         ),
         name="project_out",
-    )(attended, wo, wall, residual_in, branch_gain.reshape(1, D))
+    )(attended, far(wo), wall, far(residual_in), far(branch_gain))
 
 
 def solution(mesh):

time: 161 us -> 142 us (0.88)
  Pallas kernels: 154 us -> 139 us
  local copies, waits for them, and re-layouts: 4.8 us -> 0.83 us
    pallas_call x1, Pallas kernels: 104 us -> 93.2 us  [per_device(): pl.pallas_call(gather_kernel, out_shape=(jax.ShapeDtypeStruct((SUF, 4 * H...]
    pallas_call x1, Pallas kernels: 37.8 us -> 31 us  [per_device(): pl.pallas_call(output_kernel, out_shape=jax.ShapeDtypeStruct((TOK, D), BF...]
    unnamed x17 -> x7, local copies, waits for them, and re-layouts: 3.44 us -> 0.83 us
    pallas_call x1, Pallas kernels: 12.3 us -> 14.8 us  [per_device(): pl.pallas_call(attend_kernel, out_shape=jax.ShapeDtypeStruct((SUF, 2 * HD...]
where the time goes in v3:
time: 142 us; the launch traced here: 140 us
  Pallas kernels  139 us (98%)
    pallas_call x1, Pallas kernels, per_device(): pl.pallas_call(gather_kernel, out_shape=(jax.ShapeDtypeStruct((SUF, 4 * H...  93.2 us
    pallas_call x1, Pallas kernels, per_device(): pl.pallas_call(output_kernel, out_shape=jax.ShapeDtypeStruct((TOK, D), BF...  31 us
    pallas_call x1, Pallas kernels, per_device(): pl.pallas_call(attend_kernel, out_shape=jax.ShapeDtypeStruct((SUF, 2 * HD...  14.8 us

profile of v3, /device:TPU:40, one launch (start us, length us, event | category | flops | bytes accessed | tf_op | source)
XLA Modules:
  0.0 139.9 jit_solution(13740388039784452371)
XLA Ops:
  0.0 0.0 copy-start
  0.0 0.0 copy-start.1
  0.0 0.0 copy-start.2
  0.0 93.2 %gather_project.1 = (bf16[1024,512]{1,0:T(8,128)(2,1)S(1)}, bf16[16,128,256]{2,1,0:T(8,128)(2,1)S(1)}, bf16[4,256,4608]{2,1,0:T(8,128)(2,1)}) custom-call(bf16[64,4608]{1,0:T(8,128)(2,1)} %res_hbm.3, f32[4608]{0:T(1024)} %gain_hbm.2, bf16[9216,128]{1,0:T(8,128)(2,1)} %bitcast.6, bf16[4608,256]{1,0:T(8,128)(2,1)} %bitcast.7, bf16[256,4608]{1,0:T(8,128)(2,1)} %bitcast.4, ...), custom_call_target="tpu_custom_call" | custom-call | tf_op jit(solution)/shard_map/gather_project/pallas_call | solution.py:749
  93.2 0.0 copy-done
  93.2 0.0 copy-done.1
  93.2 0.0 copy-done.2
  93.2 14.8 %attend.1.att_ref = bf16[1024,256]{1,0:T(8,128)(2,1)S(1)} custom-call(bf16[1024,512]{1,0:T(8,128)(2,1)S(1)} %get-tuple-element.8.qkv_ref, bf16[16,128,256]{2,1,0:T(8,128)(2,1)S(1)} %get-tuple-element.9.pages_ref, s32[1,4,32]{2,1,0:T(4,128)S(1)} %copy-done, s32[1,4]{1,0:T(1,128)S(1)} %copy-done.1, s32[1,4]{1,0:T(1,128)S(1)} %copy-done.2), custom_call_target="tpu_custom_call" | custom-call | tf_op jit(solution)/shard_map/attend/pallas_call | solution.py:822
  108.0 31.0 %project_out.1 = bf16[64,4608]{1,0:T(8,128)(2,1)S(1)} custom-call(bf16[1024,256]{1,0:T(8,128)(2,1)S(1)} %attend.1.att_ref, bf16[256,4608]{1,0:T(8,128)(2,1)} %bitcast.5, bf16[4,256,4608]{2,1,0:T(8,128)(2,1)} %get-tuple-element.10.wall_hbm, bf16[64,4608]{1,0:T(8,128)(2,1)} %res_hbm.3, f32[4608]{0:T(1024)} %gain_hbm.3), custom_call_target="tpu_custom_call" | custom-call | tf_op jit(solution)/shard_map/project_out/pallas_call | solution.py:837
  139.1 0.8 copy.13
Async XLA Ops:
  0.0 93.2 %copy-start = (s32[1,4,32]{2,1,0:T(4,128)S(1)}, s32[1,4,32]{2,1,0:T(4,128)}, u32[]{:S(2)}) copy-start(s32[1,4,32]{2,1,0:T(4,128)} %own_ref.1) | copy-start | bytes 1540
  0.0 93.2 %copy-start.1 = (s32[1,4]{1,0:T(1,128)S(1)}, s32[1,4]{1,0:T(1,128)}, u32[]{:S(2)}) copy-start(s32[1,4]{1,0:T(1,128)} %ml_ref.1) | copy-start | bytes 52
  0.0 93.2 %copy-start.2 = (s32[1,4]{1,0:T(1,128)S(1)}, s32[1,4]{1,0:T(1,128)}, u32[]{:S(2)}) copy-start(s32[1,4]{1,0:T(1,128)} %sl_ref.1) | copy-start | bytes 52

commit v4 on v3

--- a/solution.py
+++ b/solution.py
@@ -157,141 +157,6 @@
     cp_wkv.start()
     cp_pool.start()
 
-    smalls[0].wait()
-    smalls[5].wait()
-    xv = res[...].astype(F32)
-    ms = jnp.mean(xv * xv, axis=-1, keepdims=True)
-    g[own_b] = (xv * lax.rsqrt(ms + 1e-06) * gain_ref[...].reshape(1, D)).astype(BF16)
-    pl.semaphore_wait(barrier, 5 + NREP - 1)
-
-    def token_copy(b):
-        return remote(g.at[b], g.at[b], ts.at[b], tr.at[b], *token_dev)
-
-    def ysend(d, b):
-        return remote(g.at[b], g.at[2 * (1 + d) + b], ys.at[d, b], yr.at[d, b], *y_dev[d])
-
-    def yrecv(d, b):
-        at = g.at[2 * (1 + d) + b]
-        return remote(at, at, ys.at[d, b], yr.at[d, b], *y_dev[d])
-
-    def yhalf(d, b):
-        rows = pl.ds(d * HALF, HALF)
-        return remote(
-            g.at[2 * (1 + d) + b, rows], g.at[6 + b, rows], yhs.at[d, b], yhr.at[d, b], *y_dev[d]
-        )
-
-    def view(item, xx, cc, half=None):
-        n = WROWS[item]
-        first = (xx * 2 + cc) * n
-        if half is not None:
-            n = n // 2
-            first = first + half * n
-        rows = pl.ds(first, n)
-        if item == 0:
-            return w2.at[rows, pl.ds(256, 256)]
-        if item == 1:
-            return raw2.at[rows]
-        return wall_ref.at[(z + (3, 1, 2)[item - 2]) % NZ, rows]
-
-    def win_send(item):
-        n = WROWS[item]
-        src = (wkv_hbm, wq_hbm)[item].at[pl.ds((x * 2 + c) * n, n)]
-        return remote(src, view(item, x, c), wis.at[item], wir.at[item], *weight_dev)
-
-    def win_recv(item):
-        at = view(item, x, c)
-        return remote(at, at, wis.at[item], wir.at[item], *weight_dev)
-
-    def wz_send(d):
-        n = WROWS[2 + d]
-        rows = pl.ds((x * 2 + c) * n, n)
-        return remote(wo_hbm.at[rows], wall_ref.at[z, rows], zs.at[d], zr.at[d], *z_dev[d])
-
-    def wz_recv(d):
-        at = view(2 + d, x, c)
-        return remote(at, at, zs.at[d], zr.at[d], *z_dev[d])
-
-    def wz_half(d):
-        at = view(2 + d, x, c, d)
-        return remote(at, at, zhs.at[d], zhr.at[d], *z_dev[d])
-
-    def wz_half_recv(d):
-        at = view(4, x, c, d)
-        return remote(at, at, zhs.at[d], zhr.at[d], *z_dev[d])
-
-    def behind(d):
-        return (x + (3 if d == 0 else 1)) % NX
-
-    def x_copy(d, item, xx):
-        at = view(item, xx, c)
-        return remote(at, at, xs.at[d, item], xr.at[d, item], *x_dev[d])
-
-    def x_half(d, item, xx):
-        at = view(item, xx, c, d)
-        return remote(at, at, xhs.at[d, item], xhr.at[d, item], *x_dev[d])
-
-    def core_copy(n, item, cc):
-        if n == 0:
-            at = view(item, x, cc)
-        elif n < 3:
-            at = view(item, behind(n - 1), cc)
-        else:
-            at = view(item, (x + 2) % NX, cc, n - 3)
-        return remote(at, at, cs.at[n, item], cr.at[n, item], *core_dev)
-
-    def spread(item):
-        for d in range(2):
-            x_copy(d, item, x).start()
-        core_copy(0, item, c).start()
-
-    def spread_on(item):
-        for d in range(2):
-            x_copy(d, item, behind(d)).wait_recv()
-            x_half(d, item, behind(d)).start()
-            core_copy(1 + d, item, c).start()
-
-    def spread_last(item):
-        for d in range(2):
-            x_half(d, item, (x + 2) % NX).wait_recv()
-            core_copy(3 + d, item, c).start()
-
-    def spread_done(item):
-        for n in range(5):
-            core_copy(n, item, 1 - c).wait_recv()
-
-    def to_of(k):
-        return rep_of((x + k // 4) % NX, (zh + k // 2 % 2) % 2, (c + k % 2) % 2)
-
-    def from_of(k):
-        return rep_of((x + NX - k // 4) % NX, (zh + k // 2 % 2) % 2, (c + k % 2) % 2)
-
-    def rq_send(k):
-        return remote(treq.at[to_of(k)], rreq.at[rep], rqs.at[k], rqr.at[k], to_of(k), tp)
-
-    def rq_recv(k):
-        at = rreq.at[from_of(k)]
-        return remote(at, at, rqs.at[k], rqr.at[k], from_of(k), tp)
-
-    def pg_send(k):
-        return remote(sbuf.at[to_of(k)], pages_ref.at[rep], pgs.at[k], pgr.at[k], to_of(k), tp)
-
-    def pg_recv(k):
-        at = pages_ref.at[from_of(k)]
-        return remote(at, at, pgs.at[k], pgr.at[k], from_of(k), tp)
-
-    def each(n0, n1, f):
-        def body(i, carry):
-            f(i)
-            return carry
-
-        lax.fori_loop(n0, n1, body, 0)
-
-    for d in range(2):
-        ysend(d, own_b).start()
-    token_copy(own_b).start()
-    win_send(0).start()
-    win_send(1).start()
-
     o_iota = lax.broadcasted_iota(I32, (NREP, NB), 0)
     b_iota = lax.broadcasted_iota(I32, (1, NB), 1)
     b_up = lax.broadcasted_iota(I32, (NB, NB), 0)
@@ -324,7 +189,141 @@
         )
     treq[...] = jnp.broadcast_to(table[:, None, :], (NREP, 8, 128))
     rreq[rep] = treq[rep]
+    smalls[0].wait()
+    smalls[5].wait()
+    xv = res[...].astype(F32)
+    ms = jnp.mean(xv * xv, axis=-1, keepdims=True)
+    g[own_b] = (xv * lax.rsqrt(ms + 1e-06) * gain_ref[...].reshape(1, D)).astype(BF16)
+    pl.semaphore_wait(barrier, 5 + NREP - 1)
+
+    def token_copy(b):
+        return remote(g.at[b], g.at[b], ts.at[b], tr.at[b], *token_dev)
+
+    def ysend(d, b):
+        return remote(g.at[b], g.at[2 * (1 + d) + b], ys.at[d, b], yr.at[d, b], *y_dev[d])
+
+    def yrecv(d, b):
+        at = g.at[2 * (1 + d) + b]
+        return remote(at, at, ys.at[d, b], yr.at[d, b], *y_dev[d])
+
+    def yhalf(d, b):
+        rows = pl.ds(d * HALF, HALF)
+        return remote(
+            g.at[2 * (1 + d) + b, rows], g.at[6 + b, rows], yhs.at[d, b], yhr.at[d, b], *y_dev[d]
+        )
+
+    def view(item, xx, cc, half=None):
+        n = WROWS[item]
+        first = (xx * 2 + cc) * n
+        if half is not None:
+            n = n // 2
+            first = first + half * n
+        rows = pl.ds(first, n)
+        if item == 0:
+            return w2.at[rows, pl.ds(256, 256)]
+        if item == 1:
+            return raw2.at[rows]
+        return wall_ref.at[(z + (3, 1, 2)[item - 2]) % NZ, rows]
+
+    def win_send(item):
+        n = WROWS[item]
+        src = (wkv_hbm, wq_hbm)[item].at[pl.ds((x * 2 + c) * n, n)]
+        return remote(src, view(item, x, c), wis.at[item], wir.at[item], *weight_dev)
+
+    def win_recv(item):
+        at = view(item, x, c)
+        return remote(at, at, wis.at[item], wir.at[item], *weight_dev)
+
+    def wz_send(d):
+        n = WROWS[2 + d]
+        rows = pl.ds((x * 2 + c) * n, n)
+        return remote(wo_hbm.at[rows], wall_ref.at[z, rows], zs.at[d], zr.at[d], *z_dev[d])
+
+    def wz_recv(d):
+        at = view(2 + d, x, c)
+        return remote(at, at, zs.at[d], zr.at[d], *z_dev[d])
+
+    def wz_half(d):
+        at = view(2 + d, x, c, d)
+        return remote(at, at, zhs.at[d], zhr.at[d], *z_dev[d])
+
+    def wz_half_recv(d):
+        at = view(4, x, c, d)
+        return remote(at, at, zhs.at[d], zhr.at[d], *z_dev[d])
+
+    def behind(d):
+        return (x + (3 if d == 0 else 1)) % NX
+
+    def x_copy(d, item, xx):
+        at = view(item, xx, c)
+        return remote(at, at, xs.at[d, item], xr.at[d, item], *x_dev[d])
+
+    def x_half(d, item, xx):
+        at = view(item, xx, c, d)
+        return remote(at, at, xhs.at[d, item], xhr.at[d, item], *x_dev[d])
+
+    def core_copy(n, item, cc):
+        if n == 0:
+            at = view(item, x, cc)
+        elif n < 3:
+            at = view(item, behind(n - 1), cc)
+        else:
+            at = view(item, (x + 2) % NX, cc, n - 3)
+        return remote(at, at, cs.at[n, item], cr.at[n, item], *core_dev)
+
+    def spread(item):
+        for d in range(2):
+            x_copy(d, item, x).start()
+        core_copy(0, item, c).start()
+
+    def spread_on(item):
+        for d in range(2):
+            x_copy(d, item, behind(d)).wait_recv()
+            x_half(d, item, behind(d)).start()
+            core_copy(1 + d, item, c).start()
+
+    def spread_last(item):
+        for d in range(2):
+            x_half(d, item, (x + 2) % NX).wait_recv()
+            core_copy(3 + d, item, c).start()
+
+    def spread_done(item):
+        for n in range(5):
+            core_copy(n, item, 1 - c).wait_recv()
+
+    def to_of(k):
+        return rep_of((x + k // 4) % NX, (zh + k // 2 % 2) % 2, (c + k % 2) % 2)
+
+    def from_of(k):
+        return rep_of((x + NX - k // 4) % NX, (zh + k // 2 % 2) % 2, (c + k % 2) % 2)
+
+    def rq_send(k):
+        return remote(treq.at[to_of(k)], rreq.at[rep], rqs.at[k], rqr.at[k], to_of(k), tp)
+
+    def rq_recv(k):
+        at = rreq.at[from_of(k)]
+        return remote(at, at, rqs.at[k], rqr.at[k], from_of(k), tp)
+
+    def pg_send(k):
+        return remote(sbuf.at[to_of(k)], pages_ref.at[rep], pgs.at[k], pgr.at[k], to_of(k), tp)
+
+    def pg_recv(k):
+        at = pages_ref.at[from_of(k)]
+        return remote(at, at, pgs.at[k], pgr.at[k], from_of(k), tp)
+
+    def each(n0, n1, f):
+        def body(i, carry):
+            f(i)
+            return carry
+
+        lax.fori_loop(n0, n1, body, 0)
+
     each(1, NREP, lambda d: rq_send(d).start())
+    win_send(1).start()
+    win_send(0).start()
+    token_copy(own_b).start()
+    for d in range(2):
+        ysend(d, own_b).start()
 
     each(1, NREP, lambda d: rq_recv(d).wait_recv())
     cp_req = pltpu.make_async_copy(rreq, sreq, loc.at[8])
@@ -366,7 +365,6 @@
         sine = jnp.sin(angle)
         stab[rows, :] = jnp.where(low, -sine, sine)
 
-    each(0, SUF // 128, tables)
 
     def split(src, dst, i):
         rows = pl.ds(pl.multiple_of(i * 1024, 1024), 1024)
@@ -412,45 +410,47 @@
             yrecv(d, b).wait_recv()
             yhalf(d, b).start()
 
-    cp_wq.wait()
-    each(0, 9, functools.partial(split, raw1, w1))
+    win_recv(1).wait_recv()
+    spread(1)
+    each(0, SUF // 128, tables)
+    win_recv(0).wait_recv()
+    spread(0)
     token_copy(pair_b).wait_recv()
     for d in range(2):
         ysend(d, pair_b).start()
-    for item in range(2):
-        win_recv(item).wait_recv()
-        spread(item)
     for d in range(2):
         wz_send(d).start()
-    each(0, 8, functools.partial(fill, 1))
+    spread_on(1)
+    cp_wq.wait()
+    each(0, 9, functools.partial(split, raw1, w1))
     ystep(own_b)
-    spread_on(0)
-    spread_on(1)
     for d in range(2):
         wz_recv(d).wait_recv()
         wz_half(d).start()
-    spread_last(0)
-    spread_last(1)
+    spread_on(0)
     for item in (2, 3):
         spread(item)
-    cp_wkv.wait()
+    each(0, 8, functools.partial(fill, 1))
+    spread_last(1)
+    spread_last(0)
+    for d in range(2):
+        wz_half_recv(d).wait_recv()
+    spread(4)
     spread_done(1)
     each(0, 9, functools.partial(split, raw2, w2))
+    cp_wkv.wait()
     spread_done(0)
     project(0, 2)
     ystep(pair_b)
-    for d in range(2):
-        wz_half_recv(d).wait_recv()
-    spread(4)
-    project(2, 4)
     for item in (2, 3):
         spread_on(item)
+    project(2, 4)
+    spread_on(4)
     for b in range(2):
         for d in range(2):
             at = g.at[6 + b, pl.ds(d * HALF, HALF)]
             remote(at, at, yhs.at[d, b], yhr.at[d, b], *y_dev[d]).wait_recv()
     project(6, 2)
-    spread_on(4)
     for item in (2, 3, 4):
         spread_last(item)
 

time: 142 us -> 133 us (0.937)
  the two profiles are of different devices: /device:TPU:40 before, /device:TPU:34 now
where the time goes in v4:
time: 133 us
  Pallas kernels  132 us (99%)
    pallas_call x1, Pallas kernels, per_device(): pl.pallas_call(gather_kernel, out_shape=(jax.ShapeDtypeStruct((SUF, 4 * H...  86.1 us
    pallas_call x1, Pallas kernels, per_device(): pl.pallas_call(output_kernel, out_shape=jax.ShapeDtypeStruct((TOK, D), BF...  29.5 us
    pallas_call x1, Pallas kernels, per_device(): pl.pallas_call(attend_kernel, out_shape=jax.ShapeDtypeStruct((SUF, 2 * HD...  16.8 us

profile of v4, /device:TPU:34, one launch (start us, length us, event | category | flops | bytes accessed | tf_op | source)
XLA Modules:
  0.0 133.3 jit_solution(6320790066753040091)
XLA Ops:
  0.0 0.0 copy-start
  0.0 0.0 copy-start.1
  0.0 0.0 copy-start.2
  0.0 86.1 %gather_project.1 = (bf16[1024,512]{1,0:T(8,128)(2,1)S(1)}, bf16[16,128,256]{2,1,0:T(8,128)(2,1)S(1)}, bf16[4,256,4608]{2,1,0:T(8,128)(2,1)}) custom-call(bf16[64,4608]{1,0:T(8,128)(2,1)} %res_hbm.3, f32[4608]{0:T(1024)} %gain_hbm.2, bf16[9216,128]{1,0:T(8,128)(2,1)} %bitcast.6, bf16[4608,256]{1,0:T(8,128)(2,1)} %bitcast.7, bf16[256,4608]{1,0:T(8,128)(2,1)} %bitcast.4, ...), custom_call_target="tpu_custom_call" | custom-call | tf_op jit(solution)/shard_map/gather_project/pallas_call | solution.py:749
  86.1 0.0 copy-done
  86.2 0.0 copy-done.1
  86.2 0.0 copy-done.2
  86.2 16.8 %attend.1.att_ref = bf16[1024,256]{1,0:T(8,128)(2,1)S(1)} custom-call(bf16[1024,512]{1,0:T(8,128)(2,1)S(1)} %get-tuple-element.8.qkv_ref, bf16[16,128,256]{2,1,0:T(8,128)(2,1)S(1)} %get-tuple-element.9.pages_ref, s32[1,4,32]{2,1,0:T(4,128)S(1)} %copy-done, s32[1,4]{1,0:T(1,128)S(1)} %copy-done.1, s32[1,4]{1,0:T(1,128)S(1)} %copy-done.2), custom_call_target="tpu_custom_call" | custom-call | tf_op jit(solution)/shard_map/attend/pallas_call | solution.py:822
  103.0 29.5 %project_out.1 = bf16[64,4608]{1,0:T(8,128)(2,1)S(1)} custom-call(bf16[1024,256]{1,0:T(8,128)(2,1)S(1)} %attend.1.att_ref, bf16[256,4608]{1,0:T(8,128)(2,1)} %bitcast.5, bf16[4,256,4608]{2,1,0:T(8,128)(2,1)} %get-tuple-element.10.wall_hbm, bf16[64,4608]{1,0:T(8,128)(2,1)} %res_hbm.3, f32[4608]{0:T(1024)} %gain_hbm.3), custom_call_target="tpu_custom_call" | custom-call | tf_op jit(solution)/shard_map/project_out/pallas_call | solution.py:837
  132.5 0.8 copy.13
Async XLA Ops:
  0.0 86.1 %copy-start = (s32[1,4,32]{2,1,0:T(4,128)S(1)}, s32[1,4,32]{2,1,0:T(4,128)}, u32[]{:S(2)}) copy-start(s32[1,4,32]{2,1,0:T(4,128)} %own_ref.1) | copy-start | bytes 1540
  0.0 86.2 %copy-start.1 = (s32[1,4]{1,0:T(1,128)S(1)}, s32[1,4]{1,0:T(1,128)}, u32[]{:S(2)}) copy-start(s32[1,4]{1,0:T(1,128)} %ml_ref.1) | copy-start | bytes 52
  0.0 86.2 %copy-start.2 = (s32[1,4]{1,0:T(1,128)S(1)}, s32[1,4]{1,0:T(1,128)}, u32[]{:S(2)}) copy-start(s32[1,4]{1,0:T(1,128)} %sl_ref.1) | copy-start | bytes 52

commit v5 on v4

--- a/solution.py
+++ b/solution.py
@@ -486,8 +486,8 @@
 def attend_kernel(
     qkv_ref, pages_ref, own_ref, ml_ref, sl_ref, o_ref, kpre, vpre, vsuf, acc, cnt
 ):
-    rows_blk = 128
-    keys_blk = 256
+    rows_blk = 256
+    keys_blk = 512
     scale = 1.0 / 600.0
     power = 50.0 / math.log(2.0)
     vsuf[:, :HD] = qkv_ref[:, 3 * HD :]
@@ -828,7 +828,7 @@
             pltpu.VMEM((REQ * NB * BLK, HD), BF16),
             pltpu.VMEM((REQ * NB * BLK, 2 * HD), BF16),
             pltpu.VMEM((SUF, 2 * HD), BF16),
-            pltpu.VMEM((256, 256), F32),
+            pltpu.VMEM((512, 256), F32),
             pltpu.SMEM((NREP,), I32),
         ],
         compiler_params=pltpu.CompilerParams(vmem_limit_bytes=32 << 20),

time: 133 us -> 129 us (0.970)
  the two profiles are of different devices: /device:TPU:34 before, /device:TPU:40 now
where the time goes in v5:
time: 129 us; the launch traced here: 128 us
  Pallas kernels  127 us (98%)
    pallas_call x1, Pallas kernels, per_device(): pl.pallas_call(gather_kernel, out_shape=(jax.ShapeDtypeStruct((SUF, 4 * H...  87.1 us
    pallas_call x1, Pallas kernels, per_device(): pl.pallas_call(output_kernel, out_shape=jax.ShapeDtypeStruct((TOK, D), BF...  30.8 us
    pallas_call x1, Pallas kernels, per_device(): pl.pallas_call(attend_kernel, out_shape=jax.ShapeDtypeStruct((SUF, 2 * HD...  8.93 us

profile of v5, /device:TPU:40, one launch (start us, length us, event | category | flops | bytes accessed | tf_op | source)
XLA Modules:
  0.0 127.7 jit_solution(13110242231611779267)
XLA Ops:
  0.0 0.0 copy-start
  0.0 0.0 copy-start.1
  0.0 0.0 copy-start.2
  0.0 87.1 %gather_project.1 = (bf16[1024,512]{1,0:T(8,128)(2,1)S(1)}, bf16[16,128,256]{2,1,0:T(8,128)(2,1)S(1)}, bf16[4,256,4608]{2,1,0:T(8,128)(2,1)}) custom-call(bf16[64,4608]{1,0:T(8,128)(2,1)} %res_hbm.3, f32[4608]{0:T(1024)} %gain_hbm.2, bf16[9216,128]{1,0:T(8,128)(2,1)} %bitcast.6, bf16[4608,256]{1,0:T(8,128)(2,1)} %bitcast.7, bf16[256,4608]{1,0:T(8,128)(2,1)} %bitcast.4, ...), custom_call_target="tpu_custom_call" | custom-call | tf_op jit(solution)/shard_map/gather_project/pallas_call | solution.py:749
  87.1 0.0 copy-done
  87.1 0.0 copy-done.1
  87.1 0.0 copy-done.2
  87.1 8.9 %attend.1.att_ref = bf16[1024,256]{1,0:T(8,128)(2,1)S(1)} custom-call(bf16[1024,512]{1,0:T(8,128)(2,1)S(1)} %get-tuple-element.8.qkv_ref, bf16[16,128,256]{2,1,0:T(8,128)(2,1)S(1)} %get-tuple-element.9.pages_ref, s32[1,4,32]{2,1,0:T(4,128)S(1)} %copy-done, s32[1,4]{1,0:T(1,128)S(1)} %copy-done.1, s32[1,4]{1,0:T(1,128)S(1)} %copy-done.2), custom_call_target="tpu_custom_call" | custom-call | tf_op jit(solution)/shard_map/attend/pallas_call | solution.py:822
  96.1 30.8 %project_out.1 = bf16[64,4608]{1,0:T(8,128)(2,1)S(1)} custom-call(bf16[1024,256]{1,0:T(8,128)(2,1)S(1)} %attend.1.att_ref, bf16[256,4608]{1,0:T(8,128)(2,1)} %bitcast.5, bf16[4,256,4608]{2,1,0:T(8,128)(2,1)} %get-tuple-element.10.wall_hbm, bf16[64,4608]{1,0:T(8,128)(2,1)} %res_hbm.3, f32[4608]{0:T(1024)} %gain_hbm.3), custom_call_target="tpu_custom_call" | custom-call | tf_op jit(solution)/shard_map/project_out/pallas_call | solution.py:837
  126.9 0.8 copy.13
Async XLA Ops:
  0.0 87.1 %copy-start = (s32[1,4,32]{2,1,0:T(4,128)S(1)}, s32[1,4,32]{2,1,0:T(4,128)}, u32[]{:S(2)}) copy-start(s32[1,4,32]{2,1,0:T(4,128)} %own_ref.1) | copy-start | bytes 1540
  0.0 87.1 %copy-start.1 = (s32[1,4]{1,0:T(1,128)S(1)}, s32[1,4]{1,0:T(1,128)}, u32[]{:S(2)}) copy-start(s32[1,4]{1,0:T(1,128)} %ml_ref.1) | copy-start | bytes 52
  0.0 87.1 %copy-start.2 = (s32[1,4]{1,0:T(1,128)S(1)}, s32[1,4]{1,0:T(1,128)}, u32[]{:S(2)}) copy-start(s32[1,4]{1,0:T(1,128)} %sl_ref.1) | copy-start | bytes 52
